TPU v7x, 32 devices: a whole 2x2x4 slice. The times are simulated.
32 devices in a mesh: gx: 4 (over z), gy: 8 (over y, x, core).
Axes of the slice: x: 2, y: 2, z: 4, core: 2. Of those that a mesh axis runs over, the one named last changes fastest.
Arguments:
- tokens: bfloat16 [2, 128, 18432], P(None, 'gy', 'gx'), may hold values from -250 to 250
- norm_gain: float32 [18432], P('gx'), may hold values from 0.25 to 1.75
- w_query: bfloat16 [18432, 12288], P('gx', 'gy'), may hold values from -0.046875 to 0.046875
- w_kv: bfloat16 [18432, 512], P('gx'), may hold values from -0.046875 to 0.046875
- w_out: bfloat16 [12288, 18432], P('gy', 'gx'), may hold values from -0.0546875 to 0.0546875
- cache_keys: bfloat16 [128, 2048, 256], P(('gx', 'gy')), may hold values from -1000 to 1000
- cache_values: bfloat16 [128, 2048, 256], P(('gx', 'gy')), may hold values from -6 to 6
- lengths: int32 [128], P(('gx', 'gy')), may hold values from 1024 to 2048, as said below
Outputs:
- attn_branch: bfloat16 [2, 128, 18432], P(None, 'gy', 'gx')
Inputs may be any that keep to these rules, and one draw needn't show every extreme that they name: `lengths`: each row's valid cache length; some row holds exactly 2048 and some exactly 1024.
All inputs are finite; a program needn't handle non-finite values.
Results may differ from a plain program's by a relative error of at most 0.02.
The roundings to bfloat16 on the way count: a program that leaves them out, or rounds other values in their place, can miss the bound.
Values may be sent and summed in bfloat16 or wider, within the bound.
A program may use at most 128 MiB of HBM per device.

v0:
```python
import jax
import jax.numpy as jnp
from jax import lax
from jax.sharding import PartitionSpec as P

D = 18432
HEADS = 48
HEAD_DIM = 256


def attend(query, keys_all, values_all, lens_here, new_keys, new_values):
    factor = query.shape[-1] ** (-0.5)
    scores_c = (
        jnp.einsum("rhd,rld->rhl", query, keys_all, preferred_element_type=jnp.float32) * factor
    )
    position = jnp.arange(keys_all.shape[1], dtype=jnp.int32)
    usable = position[None, None, :] < lens_here[:, None, None]
    scores_c = jnp.where(usable, scores_c, -1e30)
    scores_n = (
        jnp.einsum("rhd,rsd->rhs", query, new_keys, preferred_element_type=jnp.float32) * factor
    )
    highest = jnp.maximum(jnp.max(scores_c, axis=-1), jnp.max(scores_n, axis=-1))[..., None]
    exp_c = jnp.exp(scores_c - highest)
    exp_n = jnp.exp(scores_n - highest)
    totals = jnp.sum(exp_c, axis=-1, keepdims=True) + jnp.sum(exp_n, axis=-1, keepdims=True)
    weight_c = (exp_c / totals).astype(jnp.bfloat16)
    weight_n = (exp_n / totals).astype(jnp.bfloat16)
    result = jnp.einsum("rhl,rld->rhd", weight_c, values_all, preferred_element_type=jnp.float32)
    result = result + jnp.einsum(
        "rhs,rsd->rhd", weight_n, new_values, preferred_element_type=jnp.float32
    )
    return result.reshape(result.shape[0], -1).astype(jnp.bfloat16)


def per_device(tokens, norm_gain, w_query, w_kv, w_out, cache_keys, cache_values, lengths):
    local_rows = cache_keys.shape[0]
    kept_keys = []
    kept_values = []
    results = []
    for section in range(2):
        values_f = tokens[section : section + 1].astype(jnp.float32)
        feat_sums, feat_squares = lax.psum(
            (jnp.sum(values_f, axis=-1), jnp.sum(values_f * values_f, axis=-1)), "gx"
        )
        average = feat_sums / D
        spread = feat_squares / D - average * average
        scaled = (values_f - average[..., None]) * lax.rsqrt(spread[..., None] + 1e-05)
        normed = (scaled * norm_gain[None, None, :]).astype(jnp.bfloat16)
        gathered = lax.all_gather(normed, "gy", axis=1, tiled=True)
        query_part = jnp.einsum(
            "sbd,dc->sbc", gathered, w_query, preferred_element_type=jnp.float32
        )
        kv_part = jnp.einsum("sbd,dc->sbc", gathered, w_kv, preferred_element_type=jnp.float32)
        query_sum = lax.psum_scatter(query_part, "gx", scatter_dimension=1, tiled=True)
        kv_sum = lax.psum_scatter(kv_part, "gx", scatter_dimension=1, tiled=True)
        kv_sum = lax.dynamic_slice_in_dim(kv_sum, lax.axis_index("gy") * local_rows, local_rows, 1)
        key_value = kv_sum.astype(jnp.bfloat16)
        project_query_rows = lax.all_to_all(
            query_sum.astype(jnp.bfloat16), "gy", split_axis=1, concat_axis=2, tiled=True
        )
        fresh_keys = key_value[..., :HEAD_DIM]
        fresh_values = key_value[..., HEAD_DIM:]
        kept_keys.append(fresh_keys[0])
        kept_values.append(fresh_values[0])
        heads_query_rows = project_query_rows[0]
        mixed = attend(
            heads_query_rows.reshape(local_rows, HEADS, HEAD_DIM),
            cache_keys,
            cache_values,
            lengths,
            jnp.stack(kept_keys, axis=1),
            jnp.stack(kept_values, axis=1),
        )
        finish_mixed = mixed[None]
        head_cols = lax.all_to_all(finish_mixed, "gy", split_axis=2, concat_axis=1, tiled=True)
        partial_out = jnp.einsum(
            "sbc,cd->sbd",
            lax.all_gather(head_cols, "gx", axis=1, tiled=True),
            w_out,
            preferred_element_type=jnp.float32,
        )
        results.append(
            lax.psum_scatter(
                partial_out.astype(jnp.bfloat16), "gy", scatter_dimension=1, tiled=True
            )
        )
    return jnp.concatenate(results, axis=0)


def solution(mesh):
    in_specs = (
        P(None, "gy", "gx"),
        P("gx"),
        P("gx", "gy"),
        P("gx", None),
        P("gy", "gx"),
        P(("gx", "gy"), None, None),
        P(("gx", "gy"), None, None),
        P(("gx", "gy")),
    )
    out_specs = P(None, "gy", "gx")
    return jax.shard_map(
        per_device, mesh=mesh, in_specs=in_specs, out_specs=out_specs, check_vma=False
    )
```

profile of v0, /device:TPU:0, one launch (start us, length us, event | category | flops | bytes accessed | tf_op | source)
XLA Modules:
  0.0 499.6 jit_solution(1503920962960028749)
XLA Ops:
  6.5 1.2 convert_reduce_fusion.1
  7.7 13.5 %all-reduce = (f32[1,16]{1,0:T(1,128)S(1)}, f32[1,16]{1,0:T(1,128)S(1)}, f32[1,16]{1,0:T(1,128)S(1)}, f32[1,16]{1,0:T(1,128)S(1)}) all-reduce(f32[1,16]{1,0:T(1,128)S(1)} %bitcast.128, f32[1,16]{1,0:T(1,128)S(1)} %bitcast.129, f32[1,16]{1,0:T(1,128)S(1)} %bitcast.127, f32[1,16]{1,0:T(1,128)S(1)} %bitcast.126), channel_id=1, replica_groups=mesh['gx'=4,'gy'=8] {'gx'}, use_global_device_ids=true, to_apply=%region_12.13 | all-reduce | flops 64 | bytes 512 | tf_op jit(solution)/shard_map/psum | solution.py:42
  21.2 1.9 fusion.28
  23.1 0.7 all-gather.3.cloned.1.call-update
  23.9 21.6 %all-gather.5.cloned.1.call-done = bf16[1,128,4608]{2,1,0:T(8,128)(2,1)} async-done(((bf16[1,16,4608]{2,1,0:T(8,128)(2,1)}), bf16[1,128,4608]{2,1,0:T(8,128)(2,1)}) %all-gather.5.cloned.1.call-update) | async-done | bytes 1179664 | tf_op jit(solution)/shard_map/all_gather | solution.py:49
  45.5 4.2 fusion.15
  49.8 21.7 %all-gather.3.cloned.1.call-done = bf16[1,128,4608]{2,1,0:T(8,128)(2,1)} async-done(((bf16[1,16,4608]{2,1,0:T(8,128)(2,1)}), bf16[1,128,4608]{2,1,0:T(8,128)(2,1)}) %all-gather.3.cloned.1.call-update) | async-done | bytes 1179664 | tf_op jit(solution)/shard_map/all_gather | solution.py:49
  71.5 4.2 fusion.12
  75.8 8.1 %convolution_bitcast_fusion = f32[1,128,1536]{2,1,0:T(8,128)} fusion(bf16[4608,1536]{1,0:T(8,128)(2,1)} %param.10, bf16[1,128,4608]{2,1,0:T(8,128)(2,1)S(1)} %copy-done.2), kind=kOutput, calls=%fused_computation.8 | convolution fusion | flops 1811939328 | bytes 16121856 | tf_op jit(solution)/shard_map/sbd,dc->sbc/dot_general | solution.py:50
  84.0 8.0 %convolution_bitcast_fusion.1 = f32[1,128,1536]{2,1,0:T(8,128)} fusion(bf16[4608,1536]{1,0:T(8,128)(2,1)} %param.10, bf16[1,128,4608]{2,1,0:T(8,128)(2,1)S(1)} %copy-done.1), kind=kOutput, calls=%fused_computation.9 | convolution fusion | flops 1811939328 | bytes 16121856 | tf_op jit(solution)/shard_map/sbd,dc->sbc/dot_general | solution.py:50
  92.0 0.1 iota_compare_fusion
  92.1 1.4 reduce-scatter.15.cloned.1.call-done
  93.4 0.7 dynamic-slice_convert_fusion
  94.2 19.3 %reduce-scatter.9.cloned.1.call-done = f32[1,32,512]{2,1,0:T(8,128)} async-done(((f32[1,128,512]{2,1,0:T(8,128)}), f32[1,32,512]{2,1,0:T(8,128)}) %reduce-scatter.9.cloned.1.call-update) | async-done | bytes 65552 | tf_op jit(solution)/shard_map/reduce_scatter | solution.py:55
  113.5 0.7 dynamic-slice_convert_fusion.1
  114.2 23.0 %reduce-scatter.13.cloned.1.call-done = f32[1,32,1536]{2,1,0:T(8,128)} async-done(((f32[1,128,1536]{2,1,0:T(8,128)}), f32[1,32,1536]{2,1,0:T(8,128)}) %reduce-scatter.13.cloned.1.call-update) | async-done | bytes 196624 | tf_op jit(solution)/shard_map/reduce_scatter | solution.py:54
  137.3 0.9 convert_element_type.87
  138.2 0.2 copy.59
  138.4 0.5 broadcast.63
  138.9 1.2 reduce.8
  140.1 0.7 reshape.163
  140.8 3.7 all-to-all-start.2
  144.5 17.6 %reduce-scatter.7.cloned.1.call-done = f32[1,32,1536]{2,1,0:T(8,128)} async-done(((f32[1,128,1536]{2,1,0:T(8,128)}), f32[1,32,1536]{2,1,0:T(8,128)}) %reduce-scatter.7.cloned.1.call-update) | async-done | bytes 196624 | tf_op jit(solution)/shard_map/reduce_scatter | solution.py:54
  162.0 0.9 convert_element_type.77
  163.0 0.2 copy.60
  163.1 1.2 reduce.10
  164.3 0.7 reshape.167
  165.0 3.8 all-to-all-start
  168.8 0.1 reshape.164
  168.9 0.5 bitcast_reduce_fusion.1
  169.5 0.1 reshape_squeeze.7
  169.6 4.4 all-to-all-done
  174.0 0.1 reshape.168
  174.0 0.5 bitcast_reduce_fusion
  174.6 0.1 reshape_squeeze.6
  174.8 0.1 fusion.45
  174.9 3.8 fusion.44
  178.7 2.5 fusion.46
  181.3 0.1 fusion.34
  181.4 0.4 fusion.5
  181.8 0.2 fusion.36
  182.0 0.9 fusion.19
  183.0 9.9 %copy.36 = bf16[1,4,12288]{1,0,2:T(2,128)(2,1)} copy(bf16[1,4,12288]{2,1,0:T(4,128)(2,1)S(1)} %convert_element_type.92) | data formatting | bytes 196608 | tf_op jit(solution)/shard_map/convert_element_type | solution.py:32
  192.9 66.9 %reduce.9 = bf16[12288,4]{1,0:T(8,128)(2,1)S(1)} reduce(bf16[12288,1,4]{2,1,0:T(2,128)(2,1)} %bitcast.113, bf16[]{:T(256)} %broadcast.63), dimensions={1}, to_apply=%bitcast.82.reduce_sub_computation | reduce | bytes 196610
  259.8 6.9 %reshape.165 = bf16[8,2,3072]{2,1,0:T(2,128)(2,1)} reshape(bf16[12288,4]{1,0:T(8,128)(2,1)S(1)} %reduce.9) | data formatting | bytes 196608
  266.8 3.4 all-to-all-start.3
  270.2 1.8 fusion.4
  272.0 3.3 all-to-all-done.3
  275.3 8.7 %reshape.166 = bf16[12288,1,4]{2,1,0:T(2,128)(2,1)} reshape(bf16[8,2,3072]{2,1,0:T(2,128)(2,1)S(1)} %all-to-all-done.3) | data formatting | bytes 196608
  283.9 11.8 %copy.37 = bf16[1,4,12288]{2,1,0:T(4,128)(2,1)S(1)} copy(bf16[1,4,12288]{1,0,2:T(2,128)(2,1)} %bitcast.114) | data formatting | bytes 196608 | tf_op jit(solution)/shard_map/all_to_all | solution.py:75
  295.8 0.1 copy.38
  295.9 14.9 %all_gather.15 = bf16[1,128,1536]{2,1,0:T(8,128)(2,1)S(1)} all-gather(bf16[1,32,1536]{2,1,0:T(8,128)(2,1)S(1)} %all_to_all.61), channel_id=1, replica_groups=mesh['gx'=4,'gy'=8] {'gx'}, dimensions={1}, use_global_device_ids=true | all-gather | bytes 491520 | tf_op jit(solution)/shard_map/all_gather | solution.py:78
  310.8 8.3 %fusion.1 = bf16[1,128,4608]{2,1,0:T(8,128)(2,1)} fusion(bf16[1536,4608]{1,0:T(8,128)(2,1)} %param.12, bf16[1,128,1536]{2,1,0:T(8,128)(2,1)S(1)} %all_gather.15), kind=kOutput, calls=%fused_computation.3 | convolution fusion | flops 1812529152 | bytes 15728640 | tf_op jit(solution)/shard_map/sbc,cd->sbd/dot_general | solution.py:76
  319.2 3.0 fusion.18
  322.3 10.2 %copy.29 = bf16[1,4,12288]{1,0,2:T(2,128)(2,1)} copy(bf16[1,4,12288]{2,1,0:T(4,128)(2,1)S(1)} %convert_element_type.82) | data formatting | bytes 196608 | tf_op jit(solution)/shard_map/convert_element_type | solution.py:32
  332.5 66.9 %reduce.11 = bf16[12288,4]{1,0:T(8,128)(2,1)S(1)} reduce(bf16[12288,1,4]{2,1,0:T(2,128)(2,1)} %bitcast.112, bf16[]{:T(256)} %broadcast.63), dimensions={1}, to_apply=%bitcast.86.reduce_sub_computation | reduce | bytes 196610
  399.5 6.1 %reshape.169 = bf16[8,2,3072]{2,1,0:T(2,128)(2,1)S(1)} reshape(bf16[12288,4]{1,0:T(8,128)(2,1)S(1)} %reduce.11) | data formatting | bytes 196608
  405.5 7.6 %all_to_all.66 = bf16[8,2,3072]{2,1,0:T(2,128)(2,1)S(1)} all-to-all(bf16[8,2,3072]{2,1,0:T(2,128)(2,1)S(1)} %reshape.169), channel_id=1, replica_groups=mesh['gx'=4,'gy'=8] {'gy'}, dimensions={0} | all-to-all | bytes 196608 | tf_op jit(solution)/shard_map/all_to_all | solution.py:75
  413.1 8.7 %reshape.170 = bf16[12288,1,4]{2,1,0:T(2,128)(2,1)} reshape(bf16[8,2,3072]{2,1,0:T(2,128)(2,1)S(1)} %all_to_all.66) | data formatting | bytes 196608
  421.8 11.8 %copy.30 = bf16[1,4,12288]{2,1,0:T(4,128)(2,1)S(1)} copy(bf16[1,4,12288]{1,0,2:T(2,128)(2,1)} %bitcast.115) | data formatting | bytes 196608 | tf_op jit(solution)/shard_map/all_to_all | solution.py:75
  433.7 15.1 %all_gather.13 = bf16[1,128,1536]{2,1,0:T(8,128)(2,1)S(1)} all-gather(bf16[1,32,1536]{2,1,0:T(8,128)(2,1)S(1)} %all_to_all.54), channel_id=1, replica_groups=mesh['gx'=4,'gy'=8] {'gx'}, dimensions={1}, use_global_device_ids=true | all-gather | bytes 491520 | tf_op jit(solution)/shard_map/all_gather | solution.py:78
  448.9 8.1 %fusion = bf16[1,128,4608]{2,1,0:T(8,128)(2,1)} fusion(bf16[1536,4608]{1,0:T(8,128)(2,1)} %param.12, bf16[1,128,1536]{2,1,0:T(8,128)(2,1)S(1)} %all_gather.13), kind=kOutput, calls=%fused_computation.2 | convolution fusion | flops 1812529152 | bytes 15728640 | tf_op jit(solution)/shard_map/sbc,cd->sbd/dot_general | solution.py:76
  457.0 33.5 %reduce-scatter.11.cloned.1.call-done = bf16[1,16,4608]{2,1,0:T(8,128)(2,1)} async-done(((bf16[1,128,4608]{2,1,0:T(8,128)(2,1)}), bf16[1,16,4608]{2,1,0:T(8,128)(2,1)}) %reduce-scatter.11.cloned.1.call-update) | async-done | bytes 147472 | tf_op jit(solution)/shard_map/reduce_scatter | solution.py:83
  490.6 1.7 pad_maximum_fusion
  (50 shorter events, 0.9 us)
Async XLA Ops:
  6.5 39.0 %all-gather.5.cloned.1.call-start = ((), (), s32[]{:S(2)}) async-start(), calls=%async_computation.14 | async-start | bytes 1327104 | tf_op jit(solution)/shard_map/all_gather | solution.py:49
  23.1 48.4 %all-gather.3.cloned.1.call-start = ((), (), s32[]{:S(2)}) async-start(), calls=%async_computation.10 | async-start | bytes 1327104 | tf_op jit(solution)/shard_map/all_gather | solution.py:49
  23.9 69.6 %reduce-scatter.15.cloned.1.call-start = ((), (), s32[]{:S(2)}) async-start(), calls=%async_computation.16 | async-start | bytes 327680 | tf_op jit(solution)/shard_map/reduce_scatter | solution.py:55
  49.7 26.0 %copy-start.2 = (bf16[1,128,4608]{2,1,0:T(8,128)(2,1)S(1)}, bf16[1,128,4608]{2,1,0:T(8,128)(2,1)}, u32[]{:S(2)}) copy-start(bf16[1,128,4608]{2,1,0:T(8,128)(2,1)} %all-gather.5.cloned.1.call-done) | copy-start | bytes 3538948
  49.7 63.7 %reduce-scatter.9.cloned.1.call-start = ((), (), s32[]{:S(2)}) async-start(), calls=%async_computation.12 | async-start | bytes 327680 | tf_op jit(solution)/shard_map/reduce_scatter | solution.py:55
  75.7 61.6 %reduce-scatter.13.cloned.1.call-start = ((), (), s32[]{:S(2)}) async-start(), calls=%async_computation.15 | async-start | bytes 983040 | tf_op jit(solution)/shard_map/reduce_scatter | solution.py:54
  75.8 8.2 %copy-start.1 = (bf16[1,128,4608]{2,1,0:T(8,128)(2,1)S(1)}, bf16[1,128,4608]{2,1,0:T(8,128)(2,1)}, u32[]{:S(2)}) copy-start(bf16[1,128,4608]{2,1,0:T(8,128)(2,1)} %all-gather.3.cloned.1.call-done) | copy-start | bytes 3538948
  83.9 8.1 %copy-start.4 = (s32[4]{0:T(128)S(1)}, s32[4]{0:T(128)}, u32[]{:S(2)}) copy-start(s32[4]{0:T(128)} %param.15) | copy-start | bytes 52
  83.9 78.1 %reduce-scatter.7.cloned.1.call-start = ((), (), s32[]{:S(2)}) async-start(), calls=%async_computation.11 | async-start | bytes 983040 | tf_op jit(solution)/shard_map/reduce_scatter | solution.py:54
  140.8 24.2 %all-to-all-start.2 = ((bf16[8,2,3072]{2,1,0:T(2,128)(2,1)}), bf16[8,2,3072]{2,1,0:T(2,128)(2,1)S(1)}, u32[]{:S(2)}, u32[]{:S(2)}) async-start(bf16[8,2,3072]{2,1,0:T(2,128)(2,1)} %reshape.163), calls=%async_computation.6 | async-start | bytes 196608 | tf_op jit(solution)/shard_map/all_to_all | solution.py:58
  165.0 9.0 %all-to-all-start = ((bf16[8,2,3072]{2,1,0:T(2,128)(2,1)}), bf16[8,2,3072]{2,1,0:T(2,128)(2,1)S(1)}, u32[]{:S(2)}, u32[]{:S(2)}) async-start(bf16[8,2,3072]{2,1,0:T(2,128)(2,1)} %reshape.167), calls=%async_computation.1 | async-start | bytes 196608 | tf_op jit(solution)/shard_map/all_to_all | solution.py:58
  174.9 3.8 copy-start
  178.7 3.3 copy-start.5
  266.8 8.5 %all-to-all-start.3 = ((bf16[8,2,3072]{2,1,0:T(2,128)(2,1)}), bf16[8,2,3072]{2,1,0:T(2,128)(2,1)S(1)}, u32[]{:S(2)}, u32[]{:S(2)}) async-start(bf16[8,2,3072]{2,1,0:T(2,128)(2,1)} %reshape.165), calls=%async_computation.8 | async-start | bytes 196608 | tf_op jit(solution)/shard_map/all_to_all | solution.py:75
  270.1 186.9 %reduce-scatter.17.cloned.1.call-start = ((), (), s32[]{:S(2)}) async-start(), calls=%async_computation.17 | async-start | bytes 1327104 | tf_op jit(solution)/shard_map/reduce_scatter | solution.py:83
  310.8 8.4 %copy-start.3 = (f32[4,48,2048]{2,1,0:T(8,128)S(1)}, f32[4,48,2048]{2,1,0:T(8,128)}, u32[]{:S(2)}) copy-start(f32[4,48,2048]{2,1,0:T(8,128)} %get-tuple-element.32) | copy-start | bytes 4718596
  319.1 171.4 %reduce-scatter.11.cloned.1.call-start = ((), (), s32[]{:S(2)}) async-start(), calls=%async_computation.13 | async-start | bytes 1327104 | tf_op jit(solution)/shard_map/reduce_scatter | solution.py:83
Sparse Core Ops, SparseCore 0:
  23.2 22.2 all-gather.4
  47.4 24.0 all-gather.2
  73.8 19.6 reduce-scatter.14
  95.6 17.7 reduce-scatter.8
  115.6 21.5 reduce-scatter.12
  139.4 22.5 reduce-scatter.6
  319.3 33.9 reduce-scatter.16
  457.1 33.4 reduce-scatter.10
where the time goes:
time: 507 us; the launch traced here: 500 us
  waiting for transfers between devices  147 us (29%)
  other arithmetic  145 us (29%)
  local copies, waits for them, and re-layouts  79.7 us (16%)
  matrix products  51.6 us (10%)
  blocking collectives  51.1 us (10%)
  between operations  14.3 us (3%)
  starting transfers between devices  11.1 us (2%)
    unnamed x4, other arithmetic  136 us
    all_gather x2, waiting for transfers between devices, per_device(): gathered = lax.all_gather(normed, 'gy', axis=1, tiled=True)  43.3 us
    reduce_scatter x2, waiting for transfers between devices, per_device(): lax.psum_scatter(query_part, 'gx', scatter_dimension=1, tiled=True)  40.6 us
    reduce_scatter x2, waiting for transfers between devices, per_device(): lax.psum_scatter(partial_out.astype(jnp.bfloat16), 'gy', scatter_dimensio...  33.6 us
    unnamed x23, local copies, waits for them, and re-layouts  32.6 us
    all_gather x2, blocking collectives, per_device(): lax.all_gather(head_cols, 'gx', axis=1, tiled=True)  30 us
    all_to_all x6, local copies, waits for them, and re-layouts, per_device(): lax.all_to_all(finish_mixed, 'gy', split_axis=2, concat_axis=1, tiled=True)  23.8 us
    reduce_scatter x2, waiting for transfers between devices, per_device(): kv_sum = lax.psum_scatter(kv_part, 'gx', scatter_dimension=1, tiled=True)  20.7 us
  transfers between devices with their start and end apart: 11, of which 9 were waited for; matrix products, arithmetic and copies ran while one was open for 30% of the time, Pallas kernels for 0%

commit v1 on v0

v1 whole, which is shorter than its diff:
```python
import functools
import jax
import jax.numpy as jnp
from jax import lax
from jax.experimental import pallas as pl
from jax.experimental.pallas import tpu as pltpu
from jax.sharding import PartitionSpec as P

HEAD_DIM = 256
STEPS = 2


def attend_kernel(lens_ref, q_ref, kv_ref, k_ref, v_ref, o_ref, q_f, o_f):
    r = pl.program_id(0)
    rows = pl.num_programs(0)
    local = k_ref.shape[1]
    n = q_ref.shape[0] // 4

    @pl.when(r == 0)
    def _():
        q_f[0] = q_ref[:, :128].astype(jnp.float32)
        q_f[1] = q_ref[:, 128:].astype(jnp.float32)

    picked = pl.ds(r, n, stride=4)
    q = jnp.concatenate([q_f[0, picked, :], q_f[1, picked, :]], axis=1).astype(jnp.bfloat16)
    factor = HEAD_DIM ** (-0.5)
    s = lax.dot_general(
        q, k_ref[0], (((1,), (1,)), ((), ())), preferred_element_type=jnp.float32
    ) * factor
    pos = lax.broadcasted_iota(jnp.int32, s.shape, 1)
    s = jnp.where(pos < lens_ref[r], s, -1e30)
    kv = kv_ref[...].astype(jnp.float32)
    row_id = lax.broadcasted_iota(jnp.int32, kv.shape, 0)
    fresh = [
        jnp.sum(jnp.where(row_id == t * 4 + r, kv, 0.0), axis=0, keepdims=True)
        for t in range(STEPS)
    ]
    q32 = q.astype(jnp.float32)
    new = [
        jnp.sum(q32 * fresh[t][:, :HEAD_DIM], axis=1, keepdims=True) * factor
        for t in range(STEPS)
    ]
    step = lax.broadcasted_iota(jnp.int32, (n, 1), 0) % STEPS
    for t in range(1, STEPS):
        new[t] = jnp.where(step >= t, new[t], -1e30)
    top = jnp.max(s, axis=1, keepdims=True)
    for t in range(STEPS):
        top = jnp.maximum(top, new[t])
    e = jnp.exp(s - top)
    total = jnp.sum(e, axis=1, keepdims=True)
    e_new = [jnp.exp(x - top) for x in new]
    for x in e_new:
        total = total + x
    inv = 1.0 / total
    w = (e * inv).astype(jnp.bfloat16)
    out = jnp.dot(w, v_ref[0], preferred_element_type=jnp.float32)
    for t in range(STEPS):
        wt = (e_new[t] * inv).astype(jnp.bfloat16).astype(jnp.float32)
        out = out + wt * fresh[t][:, HEAD_DIM:]
    o_f[0, picked, :] = out[:, :128]
    o_f[1, picked, :] = out[:, 128:]

    @pl.when(r == rows - 1)
    def _():
        o_ref[:, :128] = o_f[0].astype(jnp.bfloat16)
        o_ref[:, 128:] = o_f[1].astype(jnp.bfloat16)


def attend(lens, q, kv, keys, values):
    rows, cache, dim = keys.shape
    whole = lambda a: pl.BlockSpec(a.shape, lambda r: (0, 0))
    return pl.pallas_call(
        attend_kernel,
        grid=(rows,),
        out_shape=jax.ShapeDtypeStruct(q.shape, jnp.bfloat16),
        in_specs=[
            pl.BlockSpec(memory_space=pltpu.SMEM),
            whole(q),
            whole(kv),
            pl.BlockSpec((1, cache, dim), lambda r: (r, 0, 0)),
            pl.BlockSpec((1, cache, dim), lambda r: (r, 0, 0)),
        ],
        out_specs=whole(q),
        scratch_shapes=[
            pltpu.VMEM((2, q.shape[0], 128), jnp.float32),
            pltpu.VMEM((2, q.shape[0], 128), jnp.float32),
        ],
        compiler_params=pltpu.CompilerParams(vmem_limit_bytes=40 * 2**20),
    )(lens, q, kv, keys, values)


def per_device(d, n_gx, n_gy, tokens, norm_gain, w_query, w_kv, w_out, keys, values, lengths):
    local = keys.shape[0]
    pack = STEPS * local
    heads = w_query.shape[1] // HEAD_DIM
    width = tokens.shape[2]
    flats = tokens.shape[1] // local
    x = tokens.reshape(STEPS, flats, local, width).transpose(1, 0, 2, 3)
    x = x.reshape(flats * pack, width).astype(jnp.float32)
    sums, squares = lax.psum((jnp.sum(x, axis=-1), jnp.sum(x * x, axis=-1)), "gx")
    average = sums / d
    spread = squares / d - average * average
    normed = (x - average[:, None]) * lax.rsqrt(spread[:, None] + 1e-05) * norm_gain[None, :]
    normed = lax.all_gather(normed.astype(jnp.bfloat16), "gy", axis=0, tiled=True)
    q = jnp.dot(normed, w_query, preferred_element_type=jnp.float32)
    q = lax.psum_scatter(q, "gx", scatter_dimension=0, tiled=True).astype(jnp.bfloat16)
    mine = lax.dynamic_index_in_dim(
        normed.reshape(n_gx, n_gy, pack, width), lax.axis_index("gy"), 1, keepdims=False
    )
    kv = jnp.dot(mine.reshape(n_gx * pack, width), w_kv, preferred_element_type=jnp.float32)
    kv = lax.psum_scatter(kv, "gx", scatter_dimension=0, tiled=True).astype(jnp.bfloat16)
    q = q.reshape(n_gy, pack, heads, HEAD_DIM).transpose(0, 2, 1, 3)
    q = q.reshape(n_gy, heads * pack, HEAD_DIM)
    q = lax.all_to_all(q, "gy", split_axis=0, concat_axis=0, tiled=True)
    mixed = attend(lengths, q.reshape(-1, HEAD_DIM), kv, keys, values)
    mixed = mixed.reshape(n_gy, heads * pack, HEAD_DIM)
    mixed = lax.all_to_all(mixed, "gy", split_axis=0, concat_axis=0, tiled=True)
    mixed = lax.all_gather(mixed, "gx", axis=0, tiled=True)
    mixed = mixed.reshape(n_gx * n_gy, heads, pack, HEAD_DIM).transpose(0, 2, 1, 3)
    mixed = mixed.reshape(n_gx * n_gy * pack, heads * HEAD_DIM)
    out = jnp.dot(mixed, w_out, preferred_element_type=jnp.float32).astype(jnp.bfloat16)
    out = lax.psum_scatter(out, "gy", scatter_dimension=0, tiled=True)
    out = out.reshape(flats, STEPS, local, width).transpose(1, 0, 2, 3)
    return out.reshape(STEPS, flats * local, width)


def solution(mesh):
    n_gx, n_gy = mesh.shape["gx"], mesh.shape["gy"]
    in_specs = (
        P(None, "gy", "gx"),
        P("gx"),
        P("gx", "gy"),
        P("gx", None),
        P("gy", "gx"),
        P(("gx", "gy"), None, None),
        P(("gx", "gy"), None, None),
        P(("gx", "gy")),
    )

    def run(tokens, norm_gain, *rest):
        d = tokens.shape[2]
        return jax.shard_map(
            functools.partial(per_device, d, n_gx, n_gy),
            mesh=mesh, in_specs=in_specs, out_specs=P(None, "gy", "gx"), check_vma=False,
        )(tokens, norm_gain, *rest)

    return run
```

time: 507 us -> 223 us (0.44); the launches traced: 500 us -> 222 us
  other arithmetic: 145 us -> 4.3 us
  local copies, waits for them, and re-layouts: 79.7 us -> 7.86 us
  matrix products: 51.6 us -> 24.9 us
  waiting for transfers between devices: 147 us -> 122 us
  blocking collectives: 51.1 us -> 40.8 us
  starting transfers between devices: 11.1 us -> 3.78 us
  Pallas kernels: 0 us -> 5.37 us
    unnamed x4 -> x0, other arithmetic: 136 us -> none
    unnamed x23 -> x6, local copies, waits for them, and re-layouts: 32.6 us -> 4.37 us
    dot_general x13 -> x3, matrix products: 51.6 us -> 24.9 us  [the longest x1 10.7 us: per_device(): q = jnp.dot(normed, w_query, preferred_element_type=jnp.float32)]
    all_to_all x12 -> x0, local copies, waits for them, and re-layouts: 24.9 us -> none  [the longest x6 23.8 us: per_device(): lax.all_to_all(finish_mixed, 'gy', split_axis=2, concat_axis=1, tiled=True)]
    convert_element_type x8 -> x3, local copies, waits for them, and re-layouts: 22 us -> 1.39 us  [per_device(): x = x.reshape(flats * pack, width).astype(jnp.float32)]
    all_gather x2 -> x1, waiting for transfers between devices: 43.3 us -> 27.3 us  [per_device(): lax.all_gather(normed.astype(jnp.bfloat16), 'gy', axis=0, tiled=True)]
    all_gather x2 -> x1, blocking collectives: 30 us -> 17.6 us  [per_device(): mixed = lax.all_gather(mixed, 'gx', axis=0, tiled=True)]
    all_to_all x3 -> x1, waiting for transfers between devices: 7.65 us -> 0.01 us  [per_device(): q = lax.all_to_all(q, 'gy', split_axis=0, concat_axis=0, tiled=True)]
  transfers between devices with their start and end apart: 11 -> 5, of which waited for: 9 -> 4; matrix products, arithmetic and copies ran while one was open for 30% -> 2% of each run, Pallas kernels for 0% -> 0%
where the time goes in v1:
time: 223 us; the launch traced here: 222 us
  waiting for transfers between devices  122 us (55%)
  blocking collectives  40.8 us (18%)
  matrix products  24.9 us (11%)
  between operations  13.2 us (6%)
  local copies, waits for them, and re-layouts  7.86 us (4%)
  Pallas kernels  5.37 us (2%)
  other arithmetic  4.3 us (2%)
  starting transfers between devices  3.78 us (2%)
    reduce_scatter x1, waiting for transfers between devices, per_device(): out = lax.psum_scatter(out, 'gy', scatter_dimension=0, tiled=True)  40.6 us
    reduce_scatter x1, waiting for transfers between devices, per_device(): lax.psum_scatter(q, 'gx', scatter_dimension=0, tiled=True)  35.4 us
    all_gather x1, waiting for transfers between devices, per_device(): lax.all_gather(normed.astype(jnp.bfloat16), 'gy', axis=0, tiled=True)  27.3 us
    reduce_scatter x1, waiting for transfers between devices, per_device(): lax.psum_scatter(kv, 'gx', scatter_dimension=0, tiled=True)  18.6 us
    all_gather x1, blocking collectives, per_device(): mixed = lax.all_gather(mixed, 'gx', axis=0, tiled=True)  17.6 us
    psum x1, blocking collectives, per_device(): lax.psum((jnp.sum(x, axis=-1), jnp.sum(x * x, axis=-1)), 'gx')  13.4 us
    dot_general x1, matrix products, per_device(): q = jnp.dot(normed, w_query, preferred_element_type=jnp.float32)  10.7 us
    dot_general x1, matrix products, per_device(): jnp.dot(mixed, w_out, preferred_element_type=jnp.float32)  10.2 us
  transfers between devices with their start and end apart: 5, of which 4 were waited for; matrix products, arithmetic and copies ran while one was open for 2% of the time, Pallas kernels for 0%

profile of v1, /device:TPU:0, one launch (start us, length us, event | category | flops | bytes accessed | tf_op | source)
XLA Modules:
  0.0 222.3 jit_solution(13242354903063674497)
XLA Ops:
  6.5 0.0 all-gather.2.cloned.1.call-start
  6.5 1.1 reshape.58
  7.7 0.3 fusion.4
  8.0 0.2 reshape.56
  8.2 0.1 reduce_sum.23
  8.3 0.1 reduce_sum.25
  8.4 13.4 %all-reduce = (f32[32]{0:T(128)S(1)}, f32[32]{0:T(128)S(1)}) all-reduce(f32[32]{0:T(128)S(1)} %reduce_sum.25, f32[32]{0:T(128)S(1)} %reduce_sum.23), channel_id=1, replica_groups=mesh['gx'=4,'gy'=8] {'gx'}, use_global_device_ids=true, to_apply=%region_3.0 | all-reduce | flops 64 | bytes 512 | tf_op jit(solution)/shard_map/psum | solution.py:100
  21.9 1.6 multiply_convert_fusion
  23.4 0.0 all-gather.2.cloned.1.call-update
  23.5 0.0 reduce-scatter.4.cloned.1.call-start
  23.5 27.3 %all-gather.2.cloned.1.call-done = bf16[256,4608]{1,0:T(8,128)(2,1)} async-done(((bf16[32,4608]{1,0:T(8,128)(2,1)}), bf16[256,4608]{1,0:T(8,128)(2,1)}) %all-gather.2.cloned.1.call-update) | async-done | bytes 2359312 | tf_op jit(solution)/shard_map/all_gather | solution.py:104
  50.8 10.7 %fusion.5 = f32[256,1536]{1,0:T(8,128)} fusion(bf16[256,4608]{1,0:T(8,128)(2,1)} %all-gather.2.cloned.1.call-done, bf16[4608,1536]{1,0:T(8,128)(2,1)} %param.10), kind=kOutput, calls=%fused_computation.11 | convolution fusion | flops 3623878656 | bytes 18087936 | tf_op jit(solution)/shard_map/dot_general | solution.py:105
  61.5 0.0 copy-start.2
  61.5 0.0 reduce-scatter.4.cloned.1.call-update
  61.6 35.4 %reduce-scatter.4.cloned.1.call-done = f32[64,1536]{1,0:T(8,128)} async-done(((f32[256,1536]{1,0:T(8,128)}), f32[64,1536]{1,0:T(8,128)}) %reduce-scatter.4.cloned.1.call-update) | async-done | bytes 393232 | tf_op jit(solution)/shard_map/reduce_scatter | solution.py:106
  97.0 1.7 convert_element_type.36
  98.7 3.7 %all-to-all-start = ((bf16[8,48,256]{2,1,0:T(8,128)(2,1)}), bf16[8,48,256]{2,1,0:T(8,128)(2,1)S(1)}, u32[]{:S(2)}, u32[]{:S(2)}) async-start(bf16[8,48,256]{2,1,0:T(8,128)(2,1)} %bitcast.3), calls=%async_computation.1 | async-start | bytes 393216 | tf_op jit(solution)/shard_map/all_to_all | solution.py:114
  102.4 0.0 reduce-scatter.6.cloned.1.call-start
  102.4 4.0 %fusion = f32[32,512]{1,0:T(8,128)} fusion(bf16[4608,512]{1,0:T(8,128)(2,1)} %param.11, bf16[4,8,8,4608]{3,2,1,0:T(8,128)(2,1)} %bitcast.34, s32[]{:T(128)S(6)} %select_n.4), kind=kOutput, calls=%fused_computation.4 | convolution fusion | flops 150994944 | bytes 5079044 | tf_op jit(solution)/shard_map/dot_general | solution.py:110
  106.4 0.0 reduce-scatter.6.cloned.1.call-update
  106.4 0.0 reduce-scatter.8.cloned.1.call-start
  106.5 18.6 %reduce-scatter.6.cloned.1.call-done = f32[8,512]{1,0:T(8,128)} async-done(((f32[32,512]{1,0:T(8,128)}), f32[8,512]{1,0:T(8,128)}) %reduce-scatter.6.cloned.1.call-update) | async-done | bytes 16400 | tf_op jit(solution)/shard_map/reduce_scatter | solution.py:111
  125.1 0.7 convert_element_type.37.kv_ref
  125.8 0.0 all-to-all-done
  125.8 0.0 copy-done.2
  125.8 0.0 copy-start
  125.8 2.2 copy-done
  128.0 0.0 copy-start.1
  128.0 2.2 copy-done.1
  130.2 5.4 %shard_map.82 = bf16[384,256]{1,0:T(8,128)(2,1)S(1)} custom-call(s32[4]{0:T(128)S(1)} %copy-done.2, bf16[384,256]{1,0:T(8,128)(2,1)S(1)} %bitcast.29, bf16[8,512]{1,0:T(8,128)(2,1)S(1)} %convert_element_type.37.kv_ref, bf16[4,2048,256]{2,1,0:T(8,128)(2,1)S(1)} %copy-done, bf16[4,2048,256]{2,1,0:T(8,128)(2,1)S(1)} %copy-done.1), custom_call_target="tpu_custom_call" | custom-call | tf_op jit(solution)/shard_map/pallas_call | solution.py:72
  135.6 9.7 %all_to_all.10 = bf16[8,48,256]{2,1,0:T(8,128)(2,1)S(1)} all-to-all(bf16[8,48,256]{2,1,0:T(8,128)(2,1)S(1)} %bitcast.30), channel_id=1, replica_groups=mesh['gx'=4,'gy'=8] {'gy'}, dimensions={0} | all-to-all | bytes 393216 | tf_op jit(solution)/shard_map/all_to_all | solution.py:117
  145.2 17.6 %all_gather.7 = bf16[32,48,256]{2,1,0:T(8,128)(2,1)S(1)} all-gather(bf16[8,48,256]{2,1,0:T(8,128)(2,1)S(1)} %all_to_all.10), channel_id=1, replica_groups=mesh['gx'=4,'gy'=8] {'gx'}, dimensions={0}, use_global_device_ids=true | all-gather | bytes 983040 | tf_op jit(solution)/shard_map/all_gather | solution.py:118
  162.9 10.2 %convolution_convert_fusion = bf16[256,4608]{1,0:T(8,128)(2,1)} fusion(bf16[256,1536]{1,0:T(8,128)(2,1)S(1)} %bitcast.33, bf16[1536,4608]{1,0:T(8,128)(2,1)} %param.12), kind=kOutput, calls=%fused_computation | convolution fusion | flops 3625058304 | bytes 17301504 | tf_op jit(solution)/shard_map/dot_general | solution.py:121
  173.1 0.0 reduce-scatter.8.cloned.1.call-update
  173.2 40.6 %reduce-scatter.8.cloned.1.call-done = bf16[32,4608]{1,0:T(8,128)(2,1)} async-done(((bf16[256,4608]{1,0:T(8,128)(2,1)}), bf16[32,4608]{1,0:T(8,128)(2,1)}) %reduce-scatter.8.cloned.1.call-update) | async-done | bytes 294928 | tf_op jit(solution)/shard_map/reduce_scatter | solution.py:122
  213.8 1.0 reshape.54
  214.8 0.1 copy.13
  214.9 0.8 reshape.55
  (2 shorter events, 0.0 us)
Async XLA Ops:
  6.5 44.3 %all-gather.2.cloned.1.call-start = ((), (), s32[]{:S(2)}) async-start(), calls=%async_computation.5 | async-start | bytes 2654208 | tf_op jit(solution)/shard_map/all_gather | solution.py:104
  23.5 73.6 %reduce-scatter.4.cloned.1.call-start = ((), (), s32[]{:S(2)}) async-start(), calls=%async_computation.6 | async-start | bytes 1966080 | tf_op jit(solution)/shard_map/reduce_scatter | solution.py:106
  61.5 64.3 %copy-start.2 = (s32[4]{0:T(128)S(1)}, s32[4]{0:T(128)}, u32[]{:S(2)}) copy-start(s32[4]{0:T(128)} %lens_ref.1) | copy-start | bytes 52
  98.7 27.1 %all-to-all-start = ((bf16[8,48,256]{2,1,0:T(8,128)(2,1)}), bf16[8,48,256]{2,1,0:T(8,128)(2,1)S(1)}, u32[]{:S(2)}, u32[]{:S(2)}) async-start(bf16[8,48,256]{2,1,0:T(8,128)(2,1)} %bitcast.3), calls=%async_computation.1 | async-start | bytes 393216 | tf_op jit(solution)/shard_map/all_to_all | solution.py:114
  102.4 22.7 %reduce-scatter.6.cloned.1.call-start = ((), (), s32[]{:S(2)}) async-start(), calls=%async_computation.7 | async-start | bytes 81920 | tf_op jit(solution)/shard_map/reduce_scatter | solution.py:111
  106.4 107.4 %reduce-scatter.8.cloned.1.call-start = ((), (), s32[]{:S(2)}) async-start(), calls=%async_computation.8 | async-start | bytes 2654208 | tf_op jit(solution)/shard_map/reduce_scatter | solution.py:122
  125.8 2.2 copy-start
  128.0 2.2 copy-start.1
Sparse Core Ops, SparseCore 0:
  23.6 27.2 all-gather.1
  61.7 35.2 reduce-scatter.3
  106.5 18.5 reduce-scatter.5
  173.3 40.4 reduce-scatter.7

commit v2 on v1

--- a/solution.py
+++ b/solution.py
@@ -89,39 +89,386 @@
     )(lens, q, kv, keys, values)
 
 
+MESH = pl.DeviceIdType.MESH
+NT = 9
+
+
+def turn(i, n):
+    return lax.rem(i + 2 * n, n)
+
+
+def remote(src, dst, send, recv, target):
+    return pltpu.make_async_remote_copy(
+        src_ref=src, dst_ref=dst, send_sem=send, recv_sem=recv,
+        device_id=target, device_id_type=MESH,
+    )
+
+
+def greet(gx, gy, n_gx, n_gy):
+    barrier = pltpu.get_barrier_semaphore()
+    for o in range(1, n_gx):
+        pl.semaphore_signal(
+            barrier, inc=1, device_id=(turn(gx + o, n_gx), gy), device_id_type=MESH
+        )
+    for o in range(1, n_gy):
+        pl.semaphore_signal(
+            barrier, inc=1, device_id=(gx, turn(gy + o, n_gy)), device_id_type=MESH
+        )
+    pl.semaphore_wait(barrier, n_gx + n_gy - 2)
+
+
+def project_kernel(
+    d, n_gx, n_gy,
+    tok_ref, gain_ref, wq_hbm, wkv_hbm, q_ref, kv_ref,
+    wq, wkv, x, xg, xkv, stats, acc, own, pb, rb, kvp, kvr, qa, qb, qr,
+    wq_sem, wkv_sem, st_s, st_r, ag_s, ag_r, sb_s, sb_r, fw_s, fw_r,
+    kv_s, kv_r, rs_s, rs_r, aa_s, aa_r,
+):
+    gx, gy = lax.axis_index("gx"), lax.axis_index("gy")
+    heads = wq.shape[0]
+    pack = kv_ref.shape[0]
+    local = pack // STEPS
+    flats = x.shape[0] // pack
+    block = n_gy * pack
+    width = x.shape[1]
+    half = n_gy // 2
+    sib = gy + 1 - 2 * lax.rem(gy, 2)
+
+    def load_q(h):
+        return pltpu.make_async_copy(
+            wq_hbm.at[:, pl.ds(h * HEAD_DIM, HEAD_DIM)], wq.at[h], wq_sem.at[h]
+        )
+
+    load_kv = pltpu.make_async_copy(wkv_hbm, wkv, wkv_sem)
+    load_kv.start()
+    for h in range(heads):
+        load_q(h).start()
+    greet(gx, gy, n_gx, n_gy)
+
+    for s in range(STEPS):
+        t = tok_ref[s].astype(jnp.float32)
+        for f in range(flats):
+            x[f * pack + s * local : f * pack + (s + 1) * local, :] = t[f * local : (f + 1) * local]
+    v = x[...]
+    lane = lax.broadcasted_iota(jnp.int32, stats.shape[1:], 1)
+    stats[gx] = jnp.where(
+        lane < 64,
+        jnp.sum(v, axis=1, keepdims=True),
+        jnp.sum(v * v, axis=1, keepdims=True),
+    )
+    sends = []
+    for o in range(1, n_gx):
+        c = remote(
+            stats.at[gx], stats.at[gx], st_s.at[o], st_r.at[o], (turn(gx + o, n_gx), gy)
+        )
+        c.start()
+        sends.append(c)
+    for o in range(1, n_gx):
+        src = turn(gx - o, n_gx)
+        remote(stats.at[src], stats.at[src], st_s.at[o], st_r.at[o], (src, gy)).wait_recv()
+    total = stats[0]
+    for g in range(1, n_gx):
+        total = total + stats[g]
+    average = total[:, 0:1] / d
+    spread = total[:, 64:65] / d - average * average
+    normed = (x[...] - average) * lax.rsqrt(spread + 1e-05) * gain_ref[...]
+    xg[gy] = normed.astype(jnp.bfloat16)
+
+    for o in range(1, half):
+        c = remote(
+            xg.at[gy], xg.at[gy], ag_s.at[o], ag_r.at[o], (gx, turn(gy + 2 * o, n_gy))
+        )
+        c.start()
+        sends.append(c)
+    c = remote(xg.at[gy], xg.at[gy], sb_s, sb_r, (gx, sib))
+    c.start()
+    sends.append(c)
+    for o in range(1, half):
+        src = turn(gy - 2 * o, n_gy)
+        remote(xg.at[src], xg.at[src], ag_s.at[o], ag_r.at[o], (gx, src)).wait_recv()
+        c = remote(xg.at[src], xg.at[src], fw_s.at[o], fw_r.at[o], (gx, sib))
+        c.start()
+        sends.append(c)
+    remote(xg.at[sib], xg.at[sib], sb_s, sb_r, (gx, sib)).wait_recv()
+    for o in range(1, half):
+        src = turn(sib - 2 * o, n_gy)
+        remote(xg.at[src], xg.at[src], fw_s.at[o], fw_r.at[o], (gx, sib)).wait_recv()
+
+    per = n_gy // flats
+    at = lax.rem(gy, flats)
+    for g in range(n_gx):
+        two = xg[g * per + gy // flats, pl.ds(pl.multiple_of(at // 2 * 2 * pack, 2 * pack), 2 * pack), :]
+        two = two.astype(jnp.float32)
+        odd = lax.rem(at, 2)
+        xkv[g * pack : (g + 1) * pack, :] = jnp.where(odd == 1, two[pack:], two[:pack])
+    load_kv.wait()
+    kv = jnp.dot(xkv[...].astype(jnp.bfloat16), wkv[...], preferred_element_type=jnp.float32)
+    for g in range(n_gx):
+        kvp[g] = kv[g * pack : (g + 1) * pack]
+    for o in range(1, n_gx):
+        dst = turn(gx + o, n_gx)
+        c = remote(kvp.at[dst], kvr.at[o], kv_s.at[o], kv_r.at[o], (dst, gy))
+        c.start()
+        sends.append(c)
+
+    chunk = width // 4
+
+    def one_head(h, carry):
+        load_q(h).wait()
+        for k in range(4):
+            part = jnp.dot(
+                xg[:, :, k * chunk : (k + 1) * chunk].reshape(-1, chunk),
+                wq[h, k * chunk : (k + 1) * chunk, :],
+                preferred_element_type=jnp.float32,
+            )
+            if k == 0:
+                acc[...] = part
+            else:
+                acc[...] += part
+        for g in range(n_gx):
+            pb[g, h] = acc[g * block : (g + 1) * block, :].astype(jnp.bfloat16)
+        own[h] = acc[pl.ds(pl.multiple_of(gx * block, block), block), :]
+        for o in range(1, n_gx):
+            dst = turn(gx + o, n_gx)
+            remote(
+                pb.at[dst, h], rb.at[o, h], rs_s.at[o, h], rs_r.at[o, h], (dst, gy)
+            ).start()
+        return carry
+
+    lax.fori_loop(0, heads, one_head, 0)
+
+    for h in range(heads):
+        got = own[h]
+        for o in range(1, n_gx):
+            remote(
+                pb.at[o, h], rb.at[o, h], rs_s.at[o, h], rs_r.at[o, h], (turn(gx + o, n_gx), gy)
+            ).wait()
+            got = got + rb[o, h].astype(jnp.float32)
+        for g in range(n_gy):
+            qa[g, h * pack : (h + 1) * pack, :] = got[g * pack : (g + 1) * pack]
+    qb[...] = qa[...].astype(jnp.bfloat16)
+    for o in range(1, n_gy):
+        dst = turn(gy + o, n_gy)
+        c = remote(qb.at[dst], qr.at[gy], aa_s.at[o], aa_r.at[o], (gx, dst))
+        c.start()
+        sends.append(c)
+    qr[gy] = qb[gy]
+    kv = kvp[gx]
+    for o in range(1, n_gx):
+        remote(
+            kvp.at[o], kvr.at[o], kv_s.at[o], kv_r.at[o], (turn(gx + o, n_gx), gy)
+        ).wait_recv()
+        kv = kv + kvr[o]
+    kv_ref[...] = kv.astype(jnp.bfloat16)
+    for o in range(1, n_gy):
+        src = turn(gy - o, n_gy)
+        remote(qb.at[src], qr.at[src], aa_s.at[o], aa_r.at[o], (gx, src)).wait_recv()
+    q_ref[...] = qr[...]
+    for c in sends:
+        c.wait_send()
+
+
+def project(d, n_gx, n_gy, local, tokens, gain, w_query, w_kv):
+    pack = STEPS * local
+    heads = w_query.shape[1] // HEAD_DIM
+    mine = tokens.shape[0] * tokens.shape[1]
+    width = tokens.shape[2]
+    block = n_gy * pack
+    dma = pltpu.SemaphoreType.DMA
+    bf, f32 = jnp.bfloat16, jnp.float32
+    vmem = pl.BlockSpec(memory_space=pltpu.VMEM)
+    return pl.pallas_call(
+        functools.partial(project_kernel, d, n_gx, n_gy),
+        out_shape=(
+            jax.ShapeDtypeStruct((n_gy, heads * pack, HEAD_DIM), bf),
+            jax.ShapeDtypeStruct((pack, w_kv.shape[1]), bf),
+        ),
+        in_specs=[vmem, vmem, pl.BlockSpec(memory_space=pl.ANY), pl.BlockSpec(memory_space=pl.ANY)],
+        out_specs=(vmem, vmem),
+        scratch_shapes=[
+            pltpu.VMEM((heads, width, HEAD_DIM), bf),
+            pltpu.VMEM(w_kv.shape, bf),
+            pltpu.VMEM((mine, width), f32),
+            pltpu.VMEM((n_gy, mine, width), bf),
+            pltpu.VMEM((n_gx * pack, width), f32),
+            pltpu.VMEM((n_gx, mine, 128), f32),
+            pltpu.VMEM((n_gy * mine, HEAD_DIM), f32),
+            pltpu.VMEM((heads, block, HEAD_DIM), f32),
+            pltpu.VMEM((n_gx, heads, block, HEAD_DIM), bf),
+            pltpu.VMEM((n_gx, heads, block, HEAD_DIM), bf),
+            pltpu.VMEM((n_gx, pack, w_kv.shape[1]), f32),
+            pltpu.VMEM((n_gx, pack, w_kv.shape[1]), f32),
+            pltpu.VMEM((n_gy, heads * pack, HEAD_DIM), f32),
+            pltpu.VMEM((n_gy, heads * pack, HEAD_DIM), bf),
+            pltpu.VMEM((n_gy, heads * pack, HEAD_DIM), bf),
+            dma((heads,)), dma,
+            dma((n_gx,)), dma((n_gx,)),
+            dma((n_gy // 2,)), dma((n_gy // 2,)),
+            dma, dma,
+            dma((n_gy // 2,)), dma((n_gy // 2,)),
+            dma((n_gx,)), dma((n_gx,)),
+            dma((n_gx, heads)), dma((n_gx, heads)),
+            dma((n_gy,)), dma((n_gy,)),
+        ],
+        compiler_params=pltpu.CompilerParams(
+            collective_id=0, has_side_effects=True, vmem_limit_bytes=56 * 2**20
+        ),
+    )(tokens, gain.reshape(1, -1), w_query, w_kv)
+
+
+def output_kernel(
+    n_gx, n_gy, pack,
+    m_ref, w_hbm, o_ref,
+    w, ab, x2f, x2b, pb, sb, keep, psum, rb, of,
+    w_sem, aa_s, aa_r, ag_s, ag_r, sib_s, sib_r, rs_s, rs_r,
+):
+    gx, gy = lax.axis_index("gx"), lax.axis_index("gy")
+    tile = w.shape[2]
+    heads = m_ref.shape[1] // pack
+    half = n_gy // 2
+    mine = x2f.shape[0] // n_gy
+    odd = lax.rem(gy, 2)
+    sib = gy + 1 - 2 * odd
+
+    def load(t):
+        return pltpu.make_async_copy(
+            w_hbm.at[:, pl.ds(t * tile, tile)], w.at[t], w_sem.at[t]
+        )
+
+    for t in range(NT):
+        load(t).start()
+    greet(gx, gy, n_gx, n_gy)
+
+    here = gx * n_gy + gy
+    sends = []
+    for o in range(1, n_gy):
+        dst = turn(gy + o, n_gy)
+        c = remote(m_ref.at[dst], ab.at[here], aa_s.at[o], aa_r.at[o], (gx, dst))
+        c.start()
+        sends.append(c)
+    ab[here] = m_ref[gy]
+    for o in range(n_gy):
+        src = turn(gy - o, n_gy)
+        slot = gx * n_gy + src
+        if o > 0:
+            remote(ab.at[slot], ab.at[slot], aa_s.at[o], aa_r.at[o], (gx, src)).wait_recv()
+        for p in range(1, n_gx):
+            c = remote(
+                ab.at[slot], ab.at[slot], ag_s.at[o, p], ag_r.at[o, p], (turn(gx + p, n_gx), gy)
+            )
+            c.start()
+            sends.append(c)
+    for o in range(n_gy):
+        for p in range(1, n_gx):
+            src = turn(gx - p, n_gx)
+            slot = src * n_gy + turn(gy - o, n_gy)
+            remote(
+                ab.at[slot], ab.at[slot], ag_s.at[o, p], ag_r.at[o, p], (src, gy)
+            ).wait_recv()
+
+    def place(g, carry):
+        got = ab[g].astype(jnp.float32)
+        for h in range(heads):
+            x2f[pl.ds(pl.multiple_of(g * pack, pack), pack), h * HEAD_DIM : (h + 1) * HEAD_DIM] = (
+                got[h * pack : (h + 1) * pack]
+            )
+        return carry
+
+    lax.fori_loop(0, n_gx * n_gy, place, 0)
+    x2b[...] = x2f[...].astype(jnp.bfloat16)
+
+    def to_sib(t):
+        return remote(pb.at[t, :, 1 - odd], sb.at[t], sib_s.at[t], sib_r.at[t], (gx, sib))
+
+    def multiply(t):
+        load(t).wait()
+        part = jnp.dot(x2b[...], w[t], preferred_element_type=jnp.float32).astype(jnp.bfloat16)
+        pb[t] = part.reshape(half, 2, mine, tile)
+        to_sib(t).start()
+
+    def to_peer(t, o):
+        dst = turn(gy + 2 * o, n_gy)
+        return remote(
+            psum.at[t, dst // 2], rb.at[t, o], rs_s.at[t, o], rs_r.at[t, o], (gx, dst)
+        )
+
+    def pair(t):
+        to_sib(t).wait()
+        both = pb[t, :, odd].astype(jnp.float32) + sb[t].astype(jnp.float32)
+        psum[t] = both.astype(jnp.bfloat16)
+        for o in range(1, half):
+            to_peer(t, o).start()
+        keep[t] = pb[t, gy // 2, odd].astype(jnp.float32) + sb[t, gy // 2].astype(jnp.float32)
+
+    multiply(0)
+
+    def stage(t, carry):
+        multiply(t)
+        pair(t - 1)
+        return carry
+
+    lax.fori_loop(1, NT, stage, 0)
+    pair(NT - 1)
+
+    local = pack // STEPS
+    for t in range(NT):
+        out = keep[t]
+        for o in range(1, half):
+            to_peer(t, o).wait()
+            out = out + rb[t, o].astype(jnp.float32)
+        for f in range(mine // pack):
+            for s in range(STEPS):
+                of[s, f * local : (f + 1) * local, t * tile : (t + 1) * tile] = (
+                    out[f * pack + s * local : f * pack + (s + 1) * local]
+                )
+    o_ref[...] = of[...].astype(jnp.bfloat16)
+    for c in sends:
+        c.wait_send()
+
+
+def project_out(n_gx, n_gy, local, mixed, w_out):
+    pack = STEPS * local
+    depth, width = w_out.shape
+    tile = width // NT
+    rows = n_gx * n_gy * pack
+    mine = rows // n_gy
+    half = n_gy // 2
+    dma = pltpu.SemaphoreType.DMA
+    bf, f32 = jnp.bfloat16, jnp.float32
+    vmem = pl.BlockSpec(memory_space=pltpu.VMEM)
+    return pl.pallas_call(
+        functools.partial(output_kernel, n_gx, n_gy, pack),
+        out_shape=jax.ShapeDtypeStruct((STEPS, mine // STEPS, width), bf),
+        in_specs=[vmem, pl.BlockSpec(memory_space=pl.ANY)],
+        out_specs=vmem,
+        scratch_shapes=[
+            pltpu.VMEM((NT, depth, tile), bf),
+            pltpu.VMEM((n_gx * n_gy,) + mixed.shape[1:], bf),
+            pltpu.VMEM((rows, depth), f32),
+            pltpu.VMEM((rows, depth), bf),
+            pltpu.VMEM((NT, half, 2, mine, tile), bf),
+            pltpu.VMEM((NT, half, mine, tile), bf),
+            pltpu.VMEM((NT, mine, tile), f32),
+            pltpu.VMEM((NT, half, mine, tile), bf),
+            pltpu.VMEM((NT, half, mine, tile), bf),
+            pltpu.VMEM((STEPS, mine // STEPS, width), f32),
+            dma((NT,)),
+            dma((n_gy,)), dma((n_gy,)),
+            dma((n_gy, n_gx)), dma((n_gy, n_gx)),
+            dma((NT,)), dma((NT,)),
+            dma((NT, half)), dma((NT, half)),
+        ],
+        compiler_params=pltpu.CompilerParams(
+            collective_id=1, has_side_effects=True, vmem_limit_bytes=56 * 2**20
+        ),
+    )(mixed, w_out)
+
+
 def per_device(d, n_gx, n_gy, tokens, norm_gain, w_query, w_kv, w_out, keys, values, lengths):
     local = keys.shape[0]
-    pack = STEPS * local
-    heads = w_query.shape[1] // HEAD_DIM
-    width = tokens.shape[2]
-    flats = tokens.shape[1] // local
-    x = tokens.reshape(STEPS, flats, local, width).transpose(1, 0, 2, 3)
-    x = x.reshape(flats * pack, width).astype(jnp.float32)
-    sums, squares = lax.psum((jnp.sum(x, axis=-1), jnp.sum(x * x, axis=-1)), "gx")
-    average = sums / d
-    spread = squares / d - average * average
-    normed = (x - average[:, None]) * lax.rsqrt(spread[:, None] + 1e-05) * norm_gain[None, :]
-    normed = lax.all_gather(normed.astype(jnp.bfloat16), "gy", axis=0, tiled=True)
-    q = jnp.dot(normed, w_query, preferred_element_type=jnp.float32)
-    q = lax.psum_scatter(q, "gx", scatter_dimension=0, tiled=True).astype(jnp.bfloat16)
-    mine = lax.dynamic_index_in_dim(
-        normed.reshape(n_gx, n_gy, pack, width), lax.axis_index("gy"), 1, keepdims=False
-    )
-    kv = jnp.dot(mine.reshape(n_gx * pack, width), w_kv, preferred_element_type=jnp.float32)
-    kv = lax.psum_scatter(kv, "gx", scatter_dimension=0, tiled=True).astype(jnp.bfloat16)
-    q = q.reshape(n_gy, pack, heads, HEAD_DIM).transpose(0, 2, 1, 3)
-    q = q.reshape(n_gy, heads * pack, HEAD_DIM)
-    q = lax.all_to_all(q, "gy", split_axis=0, concat_axis=0, tiled=True)
+    q, kv = project(d, n_gx, n_gy, local, tokens, norm_gain, w_query, w_kv)
     mixed = attend(lengths, q.reshape(-1, HEAD_DIM), kv, keys, values)
-    mixed = mixed.reshape(n_gy, heads * pack, HEAD_DIM)
-    mixed = lax.all_to_all(mixed, "gy", split_axis=0, concat_axis=0, tiled=True)
-    mixed = lax.all_gather(mixed, "gx", axis=0, tiled=True)
-    mixed = mixed.reshape(n_gx * n_gy, heads, pack, HEAD_DIM).transpose(0, 2, 1, 3)
-    mixed = mixed.reshape(n_gx * n_gy * pack, heads * HEAD_DIM)
-    out = jnp.dot(mixed, w_out, preferred_element_type=jnp.float32).astype(jnp.bfloat16)
-    out = lax.psum_scatter(out, "gy", scatter_dimension=0, tiled=True)
-    out = out.reshape(flats, STEPS, local, width).transpose(1, 0, 2, 3)
-    return out.reshape(STEPS, flats * local, width)
+    return project_out(n_gx, n_gy, local, mixed.reshape(q.shape), w_out)
 
 
 def solution(mesh):

time: 223 us -> 107 us (0.48)
  waiting for transfers between devices: 122 us -> 0 us
  Pallas kernels: 5.37 us -> 99 us
  blocking collectives: 40.8 us -> 0 us
  matrix products: 24.9 us -> 0 us
  between operations: 13.2 us -> 0.06 us
  other arithmetic: 4.3 us -> 0 us
  starting transfers between devices: 3.78 us -> 0 us
    reduce_scatter x3 -> x0, waiting for transfers between devices: 94.7 us -> none  [the longest x1 40.6 us: per_device(): out = lax.psum_scatter(out, 'gy', scatter_dimension=0, tiled=True)]
    pallas_call x0 -> x2, Pallas kernels: none -> 93.6 us  [the longest x1 52.3 us: project(): pl.pallas_call(functools.partial(project_kernel, d, n_gx, n_gy), out_shap...]
    all_gather x1 -> x0, waiting for transfers between devices: 27.3 us -> none  [per_device(): lax.all_gather(normed.astype(jnp.bfloat16), 'gy', axis=0, tiled=True)]
    dot_general x3 -> x0, matrix products: 24.9 us -> none  [the longest x1 10.7 us: per_device(): q = jnp.dot(normed, w_query, preferred_element_type=jnp.float32)]
    all_gather x1 -> x0, blocking collectives: 17.6 us -> none  [per_device(): mixed = lax.all_gather(mixed, 'gx', axis=0, tiled=True)]
    psum x1 -> x0, blocking collectives: 13.4 us -> none  [per_device(): lax.psum((jnp.sum(x, axis=-1), jnp.sum(x * x, axis=-1)), 'gx')]
    all_to_all x1 -> x0, blocking collectives: 9.68 us -> none  [per_device(): mixed = lax.all_to_all(mixed, 'gy', split_axis=0, concat_axis=0, tiled=True)]
    convert_element_type x3 -> x0, other arithmetic: 4 us -> none  [the longest x1 1.69 us: per_device(): lax.psum_scatter(q, 'gx', scatter_dimension=0, tiled=True)]
  transfers between devices with their start and end apart: 5 -> 0, of which waited for: 4 -> 0; matrix products, arithmetic and copies ran while one was open for 2% -> 0% of each run, Pallas kernels for 0% -> 0%
where the time goes in v2:
time: 107 us
  Pallas kernels  99 us (93%)
  local copies, waits for them, and re-layouts  7.52 us (7%)
    pallas_call x1, Pallas kernels, project(): pl.pallas_call(functools.partial(project_kernel, d, n_gx, n_gy), out_shap...  52.3 us
    pallas_call x1, Pallas kernels, project_out(): pl.pallas_call(functools.partial(output_kernel, n_gx, n_gy, pack), out_sh...  41.3 us
    unnamed x13, local copies, waits for them, and re-layouts  6.18 us
    pallas_call x1, Pallas kernels, attend(): pl.pallas_call(attend_kernel, grid=(rows,), out_shape=jax.ShapeDtypeStruc...  5.37 us

profile of v2, /device:TPU:0, one launch (start us, length us, event | category | flops | bytes accessed | tf_op | source)
XLA Modules:
  0.0 106.5 jit_solution(7249865439981006110)
XLA Ops:
  0.0 1.3 %reshape.9.gain_ref = f32[1,4608]{1,0:T(1,128)} reshape(f32[4608]{0:T(1024)} %param.9) | data formatting | bytes 36864 | tf_op jit(solution)/shard_map/reshape | solution.py:316
  1.3 0.0 copy-start
  1.3 0.0 copy-start.5
  1.4 52.3 %shard_map.82 = (bf16[8,48,256]{2,1,0:T(8,128)(2,1)}, bf16[8,512]{1,0:T(8,128)(2,1)}) custom-call(bf16[2,16,4608]{2,1,0:T(8,128)(2,1)} %tok_ref.1, f32[1,4608]{1,0:T(1,128)} %reshape.9.gain_ref, bf16[4608,1536]{1,0:T(8,128)(2,1)} %wq_hbm.1, bf16[4608,512]{1,0:T(8,128)(2,1)} %wkv_hbm.1), custom_call_target="tpu_custom_call" | custom-call | tf_op jit(solution)/shard_map/pallas_call | solution.py:280
  53.6 0.0 copy-done
  53.6 0.0 copy-done.5
  53.6 0.0 copy-start.1
  53.7 2.2 %copy-done.1 = bf16[4,2048,256]{2,1,0:T(8,128)(2,1)S(1)} copy-done((bf16[4,2048,256]{2,1,0:T(8,128)(2,1)S(1)}, bf16[4,2048,256]{2,1,0:T(8,128)(2,1)}, u32[]{:S(2)}) %copy-start.1) | copy-done | bytes 4194328
  55.8 0.0 copy-start.3
  55.8 0.9 copy-done.3
  56.8 0.0 copy-start.4
  56.8 0.7 copy-done.4
  57.5 5.4 %shard_map.83 = bf16[384,256]{1,0:T(8,128)(2,1)S(1)} custom-call(s32[4]{0:T(128)S(1)} %copy-done.5, bf16[384,256]{1,0:T(8,128)(2,1)S(1)} %bitcast.3, bf16[8,512]{1,0:T(8,128)(2,1)S(1)} %copy-done.4, bf16[4,2048,256]{2,1,0:T(8,128)(2,1)S(1)} %copy-done, bf16[4,2048,256]{2,1,0:T(8,128)(2,1)S(1)} %copy-done.1), custom_call_target="tpu_custom_call" | custom-call | tf_op jit(solution)/shard_map/pallas_call | solution.py:72
  62.8 0.0 copy-start.2
  62.9 0.7 copy-done.2
  63.5 41.3 %shard_map.84 = bf16[2,16,4608]{2,1,0:T(8,128)(2,1)} custom-call(bf16[8,48,256]{2,1,0:T(8,128)(2,1)} %bitcast.2, bf16[1536,4608]{1,0:T(8,128)(2,1)} %w_hbm.1), custom_call_target="tpu_custom_call" | custom-call | tf_op jit(solution)/shard_map/pallas_call | solution.py:439
  104.8 1.7 %copy.10 = bf16[2,16,4608]{2,1,0:T(8,128)(2,1)} copy(bf16[2,16,4608]{2,1,0:T(8,128)(2,1)} %shard_map.84) | data formatting | bytes 589824
Async XLA Ops:
  1.3 52.3 %copy-start = (bf16[4,2048,256]{2,1,0:T(8,128)(2,1)S(1)}, bf16[4,2048,256]{2,1,0:T(8,128)(2,1)}, u32[]{:S(2)}) copy-start(bf16[4,2048,256]{2,1,0:T(8,128)(2,1)} %k_ref.1) | copy-start | bytes 12582916
  1.3 52.3 %copy-start.5 = (s32[4]{0:T(128)S(1)}, s32[4]{0:T(128)}, u32[]{:S(2)}) copy-start(s32[4]{0:T(128)} %lens_ref.1) | copy-start | bytes 52
  53.6 2.2 %copy-start.1 = (bf16[4,2048,256]{2,1,0:T(8,128)(2,1)S(1)}, bf16[4,2048,256]{2,1,0:T(8,128)(2,1)}, u32[]{:S(2)}) copy-start(bf16[4,2048,256]{2,1,0:T(8,128)(2,1)} %v_ref.1) | copy-start | bytes 12582916
  55.8 0.9 copy-start.3
  56.8 0.7 copy-start.4
  62.8 0.7 copy-start.2

commit v3 on v2

--- a/solution.py
+++ b/solution.py
@@ -85,7 +85,7 @@
             pltpu.VMEM((2, q.shape[0], 128), jnp.float32),
             pltpu.VMEM((2, q.shape[0], 128), jnp.float32),
         ],
-        compiler_params=pltpu.CompilerParams(vmem_limit_bytes=40 * 2**20),
+        compiler_params=pltpu.CompilerParams(vmem_limit_bytes=58 * 2**20),
     )(lens, q, kv, keys, values)
 
 
@@ -120,19 +120,22 @@
 def project_kernel(
     d, n_gx, n_gy,
     tok_ref, gain_ref, wq_hbm, wkv_hbm, q_ref, kv_ref,
-    wq, wkv, x, xg, xkv, stats, acc, own, pb, rb, kvp, kvr, qa, qb, qr,
+    wq, wkv, xg, xkv, stats, acc, sb, rr, rl, kvp, kvr, qa, qb, qr,
     wq_sem, wkv_sem, st_s, st_r, ag_s, ag_r, sb_s, sb_r, fw_s, fw_r,
-    kv_s, kv_r, rs_s, rs_r, aa_s, aa_r,
+    kv_s, kv_r, ri_s, ri_r, le_s, le_r, aa_s, aa_r,
 ):
     gx, gy = lax.axis_index("gx"), lax.axis_index("gy")
     heads = wq.shape[0]
     pack = kv_ref.shape[0]
     local = pack // STEPS
-    flats = x.shape[0] // pack
-    block = n_gy * pack
-    width = x.shape[1]
+    width = tok_ref.shape[2]
+    rows = tok_ref.shape[1]
+    flats = rows // local
+    block = n_gy * local
+    units = STEPS * heads
     half = n_gy // 2
     sib = gy + 1 - 2 * lax.rem(gy, 2)
+    last = n_gx - 1
 
     def load_q(h):
         return pltpu.make_async_copy(
@@ -140,22 +143,19 @@
         )
 
     load_kv = pltpu.make_async_copy(wkv_hbm, wkv, wkv_sem)
-    load_kv.start()
     for h in range(heads):
         load_q(h).start()
+    load_kv.start()
     greet(gx, gy, n_gx, n_gy)
 
+    lane = lax.broadcasted_iota(jnp.int32, (rows, 128), 1)
     for s in range(STEPS):
-        t = tok_ref[s].astype(jnp.float32)
-        for f in range(flats):
-            x[f * pack + s * local : f * pack + (s + 1) * local, :] = t[f * local : (f + 1) * local]
-    v = x[...]
-    lane = lax.broadcasted_iota(jnp.int32, stats.shape[1:], 1)
-    stats[gx] = jnp.where(
-        lane < 64,
-        jnp.sum(v, axis=1, keepdims=True),
-        jnp.sum(v * v, axis=1, keepdims=True),
-    )
+        v = tok_ref[s].astype(jnp.float32)
+        stats[gx, s * rows : (s + 1) * rows, :] = jnp.where(
+            lane < 64,
+            jnp.sum(v, axis=1, keepdims=True),
+            jnp.sum(v * v, axis=1, keepdims=True),
+        )
     sends = []
     for o in range(1, n_gx):
         c = remote(
@@ -169,55 +169,90 @@
     total = stats[0]
     for g in range(1, n_gx):
         total = total + stats[g]
-    average = total[:, 0:1] / d
-    spread = total[:, 64:65] / d - average * average
-    normed = (x[...] - average) * lax.rsqrt(spread + 1e-05) * gain_ref[...]
-    xg[gy] = normed.astype(jnp.bfloat16)
-
-    for o in range(1, half):
-        c = remote(
-            xg.at[gy], xg.at[gy], ag_s.at[o], ag_r.at[o], (gx, turn(gy + 2 * o, n_gy))
-        )
-        c.start()
-        sends.append(c)
-    c = remote(xg.at[gy], xg.at[gy], sb_s, sb_r, (gx, sib))
-    c.start()
-    sends.append(c)
-    for o in range(1, half):
+
+    def to_chip(s, o):
+        return remote(
+            xg.at[s, gy], xg.at[s, gy], ag_s.at[s, o], ag_r.at[s, o],
+            (gx, turn(gy + 2 * o, n_gy)),
+        )
+
+    def to_sib(s):
+        return remote(xg.at[s, gy], xg.at[s, gy], sb_s.at[s], sb_r.at[s], (gx, sib))
+
+    def pass_on(s, o):
         src = turn(gy - 2 * o, n_gy)
-        remote(xg.at[src], xg.at[src], ag_s.at[o], ag_r.at[o], (gx, src)).wait_recv()
-        c = remote(xg.at[src], xg.at[src], fw_s.at[o], fw_r.at[o], (gx, sib))
-        c.start()
-        sends.append(c)
-    remote(xg.at[sib], xg.at[sib], sb_s, sb_r, (gx, sib)).wait_recv()
-    for o in range(1, half):
-        src = turn(sib - 2 * o, n_gy)
-        remote(xg.at[src], xg.at[src], fw_s.at[o], fw_r.at[o], (gx, sib)).wait_recv()
-
-    per = n_gy // flats
-    at = lax.rem(gy, flats)
-    for g in range(n_gx):
-        two = xg[g * per + gy // flats, pl.ds(pl.multiple_of(at // 2 * 2 * pack, 2 * pack), 2 * pack), :]
-        two = two.astype(jnp.float32)
-        odd = lax.rem(at, 2)
-        xkv[g * pack : (g + 1) * pack, :] = jnp.where(odd == 1, two[pack:], two[:pack])
-    load_kv.wait()
-    kv = jnp.dot(xkv[...].astype(jnp.bfloat16), wkv[...], preferred_element_type=jnp.float32)
-    for g in range(n_gx):
-        kvp[g] = kv[g * pack : (g + 1) * pack]
-    for o in range(1, n_gx):
+        return remote(xg.at[s, src], xg.at[s, src], fw_s.at[s, o], fw_r.at[s, o], (gx, sib))
+
+    def relay(s):
+        for o in range(1, half):
+            src = turn(gy - 2 * o, n_gy)
+            remote(
+                xg.at[s, src], xg.at[s, src], ag_s.at[s, o], ag_r.at[s, o], (gx, src)
+            ).wait_recv()
+            pass_on(s, o).start()
+
+    def arrived(s):
+        remote(xg.at[s, sib], xg.at[s, sib], sb_s.at[s], sb_r.at[s], (gx, sib)).wait_recv()
+        for o in range(1, half):
+            src = turn(sib - 2 * o, n_gy)
+            remote(
+                xg.at[s, src], xg.at[s, src], fw_s.at[s, o], fw_r.at[s, o], (gx, sib)
+            ).wait_recv()
+
+    for s in range(STEPS):
+        t = total[s * rows : (s + 1) * rows]
+        average = t[:, 0:1] / d
+        spread = t[:, 64:65] / d - average * average
+        normed = (tok_ref[s].astype(jnp.float32) - average) * lax.rsqrt(spread + 1e-05)
+        xg[s, gy] = (normed * gain_ref[...]).astype(jnp.bfloat16)
+        for o in range(1, half):
+            to_chip(s, o).start()
+        to_sib(s).start()
+    relay(0)
+    arrived(0)
+
+    def send_kv(o):
         dst = turn(gx + o, n_gx)
-        c = remote(kvp.at[dst], kvr.at[o], kv_s.at[o], kv_r.at[o], (dst, gy))
-        c.start()
-        sends.append(c)
+        return remote(kvp.at[dst], kvr.at[o], kv_s.at[o], kv_r.at[o], (dst, gy))
+
+    def fresh():
+        per = n_gy // flats
+        at = lax.rem(gy, flats)
+        for g in range(n_gx):
+            for s in range(STEPS):
+                all_rows = xg[s, g * per + gy // flats].astype(jnp.float32)
+                picked = all_rows[:local]
+                for f in range(1, flats):
+                    picked = jnp.where(at == f, all_rows[f * local : (f + 1) * local], picked)
+                xkv[g * pack + s * local : g * pack + (s + 1) * local, :] = picked
+        load_kv.wait()
+        kv = jnp.dot(xkv[...].astype(jnp.bfloat16), wkv[...], preferred_element_type=jnp.float32)
+        for g in range(n_gx):
+            kvp[g] = kv[g * pack : (g + 1) * pack]
+        for o in range(1, n_gx):
+            send_kv(o).start()
 
     chunk = width // 4
 
-    def one_head(h, carry):
-        load_q(h).wait()
+    def product(it):
+        s = it // heads
+        h = it - s * heads
+
+        @pl.when(it == heads // 2)
+        def _():
+            relay(1)
+
+        @pl.when(it == heads)
+        def _():
+            arrived(1)
+
+        @pl.when(it < heads)
+        def _():
+            load_q(h).wait()
+
         for k in range(4):
             part = jnp.dot(
-                xg[:, :, k * chunk : (k + 1) * chunk].reshape(-1, chunk),
+                xg[s, :, :, k * chunk : (k + 1) * chunk].reshape(-1, chunk),
                 wq[h, k * chunk : (k + 1) * chunk, :],
                 preferred_element_type=jnp.float32,
             )
@@ -226,26 +261,83 @@
             else:
                 acc[...] += part
         for g in range(n_gx):
-            pb[g, h] = acc[g * block : (g + 1) * block, :].astype(jnp.bfloat16)
-        own[h] = acc[pl.ds(pl.multiple_of(gx * block, block), block), :]
-        for o in range(1, n_gx):
-            dst = turn(gx + o, n_gx)
-            remote(
-                pb.at[dst, h], rb.at[o, h], rs_s.at[o, h], rs_r.at[o, h], (dst, gy)
-            ).start()
+            sb[it, g] = acc[g * block : (g + 1) * block, :]
+
+    def go_right(u, g):
+        return remote(
+            sb.at[u, g], rr.at[u, g], ri_s.at[u, g], ri_r.at[u, g], (turn(gx + 1, n_gx), gy)
+        )
+
+    def go_left(u, g):
+        return remote(
+            sb.at[u, g], rl.at[u, g], le_s.at[u, g], le_r.at[u, g], (turn(gx - 1, n_gx), gy)
+        )
+
+    def one(it, carry):
+        @pl.when(it < units)
+        def _():
+            product(it)
+
+        ur = it - gx
+
+        @pl.when((ur >= 0) & (ur < units))
+        def _():
+            for g in reversed(range(1, n_gx)):
+                @pl.when(gx < g)
+                def _():
+                    @pl.when(gx > 0)
+                    def _():
+                        go_right(ur, g).wait_recv()
+                        sb[ur, g] += rr[ur, g]
+
+                    go_right(ur, g).start()
+
+        ul = it - (last - gx)
+
+        @pl.when((ul >= 0) & (ul < units))
+        def _():
+            for g in range(last):
+                @pl.when(gx > g)
+                def _():
+                    @pl.when(gx < last)
+                    def _():
+                        go_left(ul, g).wait_recv()
+                        sb[ul, g] += rl[ul, g]
+
+                    go_left(ul, g).start()
+
+        @pl.when(it == units)
+        def _():
+            fresh()
+
         return carry
 
-    lax.fori_loop(0, heads, one_head, 0)
-
-    for h in range(heads):
-        got = own[h]
-        for o in range(1, n_gx):
-            remote(
-                pb.at[o, h], rb.at[o, h], rs_s.at[o, h], rs_r.at[o, h], (turn(gx + o, n_gx), gy)
-            ).wait()
-            got = got + rb[o, h].astype(jnp.float32)
+    lax.fori_loop(0, units + last, one, 0)
+
+    def finish(h, carry):
+        got = []
+        for s in range(STEPS):
+            u = s * heads + h
+
+            @pl.when(gx > 0)
+            def _():
+                go_right(u, gx).wait_recv()
+                sb[u, gx] += rr[u, gx]
+
+            @pl.when(gx < last)
+            def _():
+                go_left(u, gx).wait_recv()
+                sb[u, gx] += rl[u, gx]
+
+            got.append(sb[u, gx])
+        at = pl.ds(pl.multiple_of(h * pack, pack), pack)
         for g in range(n_gy):
-            qa[g, h * pack : (h + 1) * pack, :] = got[g * pack : (g + 1) * pack]
+            qa[g, at, :] = jnp.concatenate(
+                [x[g * local : (g + 1) * local] for x in got], axis=0
+            )
+        return carry
+
+    lax.fori_loop(0, heads, finish, 0)
     qb[...] = qa[...].astype(jnp.bfloat16)
     for o in range(1, n_gy):
         dst = turn(gy + o, n_gy)
@@ -255,15 +347,34 @@
     qr[gy] = qb[gy]
     kv = kvp[gx]
     for o in range(1, n_gx):
-        remote(
-            kvp.at[o], kvr.at[o], kv_s.at[o], kv_r.at[o], (turn(gx + o, n_gx), gy)
-        ).wait_recv()
+        send_kv(o).wait_recv()
         kv = kv + kvr[o]
     kv_ref[...] = kv.astype(jnp.bfloat16)
+
+    def sent(u, carry):
+        for g in range(n_gx):
+            @pl.when(gx < g)
+            def _():
+                go_right(u, g).wait_send()
+
+            @pl.when(gx > g)
+            def _():
+                go_left(u, g).wait_send()
+
+        return carry
+
+    lax.fori_loop(0, units, sent, 0)
     for o in range(1, n_gy):
         src = turn(gy - o, n_gy)
         remote(qb.at[src], qr.at[src], aa_s.at[o], aa_r.at[o], (gx, src)).wait_recv()
     q_ref[...] = qr[...]
+    for s in range(STEPS):
+        to_sib(s).wait_send()
+        for o in range(1, half):
+            to_chip(s, o).wait_send()
+            pass_on(s, o).wait_send()
+    for o in range(1, n_gx):
+        send_kv(o).wait_send()
     for c in sends:
         c.wait_send()
 
@@ -271,12 +382,13 @@
 def project(d, n_gx, n_gy, local, tokens, gain, w_query, w_kv):
     pack = STEPS * local
     heads = w_query.shape[1] // HEAD_DIM
-    mine = tokens.shape[0] * tokens.shape[1]
-    width = tokens.shape[2]
-    block = n_gy * pack
+    rows, width = tokens.shape[1:]
+    mine = STEPS * rows
+    units = STEPS * heads
     dma = pltpu.SemaphoreType.DMA
     bf, f32 = jnp.bfloat16, jnp.float32
     vmem = pl.BlockSpec(memory_space=pltpu.VMEM)
+    travel = pltpu.VMEM((units, n_gx, n_gy * local, HEAD_DIM), f32)
     return pl.pallas_call(
         functools.partial(project_kernel, d, n_gx, n_gy),
         out_shape=(
@@ -288,14 +400,11 @@
         scratch_shapes=[
             pltpu.VMEM((heads, width, HEAD_DIM), bf),
             pltpu.VMEM(w_kv.shape, bf),
-            pltpu.VMEM((mine, width), f32),
-            pltpu.VMEM((n_gy, mine, width), bf),
+            pltpu.VMEM((STEPS, n_gy, rows, width), bf),
             pltpu.VMEM((n_gx * pack, width), f32),
             pltpu.VMEM((n_gx, mine, 128), f32),
-            pltpu.VMEM((n_gy * mine, HEAD_DIM), f32),
-            pltpu.VMEM((heads, block, HEAD_DIM), f32),
-            pltpu.VMEM((n_gx, heads, block, HEAD_DIM), bf),
-            pltpu.VMEM((n_gx, heads, block, HEAD_DIM), bf),
+            pltpu.VMEM((n_gy * rows, HEAD_DIM), f32),
+            travel, travel, travel,
             pltpu.VMEM((n_gx, pack, w_kv.shape[1]), f32),
             pltpu.VMEM((n_gx, pack, w_kv.shape[1]), f32),
             pltpu.VMEM((n_gy, heads * pack, HEAD_DIM), f32),
@@ -303,11 +412,12 @@
             pltpu.VMEM((n_gy, heads * pack, HEAD_DIM), bf),
             dma((heads,)), dma,
             dma((n_gx,)), dma((n_gx,)),
-            dma((n_gy // 2,)), dma((n_gy // 2,)),
-            dma, dma,
-            dma((n_gy // 2,)), dma((n_gy // 2,)),
+            dma((STEPS, n_gy // 2)), dma((STEPS, n_gy // 2)),
+            dma((STEPS,)), dma((STEPS,)),
+            dma((STEPS, n_gy // 2)), dma((STEPS, n_gy // 2)),
             dma((n_gx,)), dma((n_gx,)),
-            dma((n_gx, heads)), dma((n_gx, heads)),
+            dma((units, n_gx)), dma((units, n_gx)),
+            dma((units, n_gx)), dma((units, n_gx)),
             dma((n_gy,)), dma((n_gy,)),
         ],
         compiler_params=pltpu.CompilerParams(
@@ -320,7 +430,7 @@
     n_gx, n_gy, pack,
     m_ref, w_hbm, o_ref,
     w, ab, x2f, x2b, pb, sb, keep, psum, rb, of,
-    w_sem, aa_s, aa_r, ag_s, ag_r, sib_s, sib_r, rs_s, rs_r,
+    w_sem, aa_s, aa_r, ri_s, ri_r, le_s, le_r, sib_s, sib_r, rs_s, rs_r,
 ):
     gx, gy = lax.axis_index("gx"), lax.axis_index("gy")
     tile = w.shape[2]
@@ -347,24 +457,58 @@
         c.start()
         sends.append(c)
     ab[here] = m_ref[gy]
-    for o in range(n_gy):
-        src = turn(gy - o, n_gy)
-        slot = gx * n_gy + src
-        if o > 0:
-            remote(ab.at[slot], ab.at[slot], aa_s.at[o], aa_r.at[o], (gx, src)).wait_recv()
-        for p in range(1, n_gx):
-            c = remote(
-                ab.at[slot], ab.at[slot], ag_s.at[o, p], ag_r.at[o, p], (turn(gx + p, n_gx), gy)
-            )
-            c.start()
-            sends.append(c)
-    for o in range(n_gy):
-        for p in range(1, n_gx):
-            src = turn(gx - p, n_gx)
-            slot = src * n_gy + turn(gy - o, n_gy)
-            remote(
-                ab.at[slot], ab.at[slot], ag_s.at[o, p], ag_r.at[o, p], (src, gy)
-            ).wait_recv()
+    last = n_gx - 1
+
+    def right(o, e):
+        slot = (gx - e) * n_gy + turn(gy - o, n_gy)
+        return remote(
+            ab.at[slot], ab.at[slot], ri_s.at[o, e], ri_r.at[o, e], (turn(gx + 1, n_gx), gy)
+        )
+
+    def left(o, e):
+        slot = (gx + e) * n_gy + turn(gy - o, n_gy)
+        return remote(
+            ab.at[slot], ab.at[slot], le_s.at[o, e], le_r.at[o, e], (turn(gx - 1, n_gx), gy)
+        )
+
+    def came_right(o, e):
+        slot = (gx - e) * n_gy + turn(gy - o, n_gy)
+        return remote(
+            ab.at[slot], ab.at[slot], ri_s.at[o, e - 1], ri_r.at[o, e - 1],
+            (turn(gx - 1, n_gx), gy),
+        )
+
+    def came_left(o, e):
+        slot = (gx + e) * n_gy + turn(gy - o, n_gy)
+        return remote(
+            ab.at[slot], ab.at[slot], le_s.at[o, e - 1], le_r.at[o, e - 1],
+            (turn(gx + 1, n_gx), gy),
+        )
+
+    for e in range(n_gx):
+        for o in range(n_gy):
+            if e == 0 and o > 0:
+                src = turn(gy - o, n_gy)
+                slot = gx * n_gy + src
+                remote(ab.at[slot], ab.at[slot], aa_s.at[o], aa_r.at[o], (gx, src)).wait_recv()
+
+            @pl.when(gx >= e)
+            def _():
+                if e > 0:
+                    came_right(o, e).wait_recv()
+
+                @pl.when(gx < last)
+                def _():
+                    right(o, e).start()
+
+            @pl.when(gx + e <= last)
+            def _():
+                if e > 0:
+                    came_left(o, e).wait_recv()
+
+                @pl.when(gx > 0)
+                def _():
+                    left(o, e).start()
 
     def place(g, carry):
         got = ab[g].astype(jnp.float32)
@@ -422,6 +566,16 @@
                     out[f * pack + s * local : f * pack + (s + 1) * local]
                 )
     o_ref[...] = of[...].astype(jnp.bfloat16)
+    for e in range(n_gx):
+        for o in range(n_gy):
+            @pl.when((gx >= e) & (gx < last))
+            def _():
+                right(o, e).wait_send()
+
+            @pl.when((gx + e <= last) & (gx > 0))
+            def _():
+                left(o, e).wait_send()
+
     for c in sends:
         c.wait_send()
 
@@ -455,6 +609,7 @@
             dma((NT,)),
             dma((n_gy,)), dma((n_gy,)),
             dma((n_gy, n_gx)), dma((n_gy, n_gx)),
+            dma((n_gy, n_gx)), dma((n_gy, n_gx)),
             dma((NT,)), dma((NT,)),
             dma((NT, half)), dma((NT, half)),
         ],

time: 107 us -> 111 us (1.037)
  Pallas kernels: 99 us -> 107 us
  local copies, waits for them, and re-layouts: 7.52 us -> 3.04 us
    pallas_call x1, Pallas kernels: 52.3 us -> 60.8 us  [project(): pl.pallas_call(functools.partial(project_kernel, d, n_gx, n_gy), out_shap...]
    unnamed x13 -> x1, local copies, waits for them, and re-layouts: 6.18 us -> 1.69 us
    pallas_call x1, Pallas kernels: 41.3 us -> 39.1 us  [project_out(): pl.pallas_call(functools.partial(output_kernel, n_gx, n_gy, pack), out_sh...]
    pallas_call x1, Pallas kernels: 5.37 us -> 7.56 us  [attend(): pl.pallas_call(attend_kernel, grid=(rows,), out_shape=jax.ShapeDtypeStruc...]
where the time goes in v3:
time: 111 us; the launch traced here: 110 us
  Pallas kernels  107 us (96%)
  local copies, waits for them, and re-layouts  3.04 us (3%)
    pallas_call x1, Pallas kernels, project(): pl.pallas_call(functools.partial(project_kernel, d, n_gx, n_gy), out_shap...  60.8 us
    pallas_call x1, Pallas kernels, project_out(): pl.pallas_call(functools.partial(output_kernel, n_gx, n_gy, pack), out_sh...  39.1 us
    pallas_call x1, Pallas kernels, attend(): pl.pallas_call(attend_kernel, grid=(rows,), out_shape=jax.ShapeDtypeStruc...  7.56 us

profile of v3, /device:TPU:0, one launch (start us, length us, event | category | flops | bytes accessed | tf_op | source)
XLA Modules:
  0.0 110.5 jit_solution(8724280460556905503)
XLA Ops:
  0.0 1.3 %reshape.9.gain_ref = f32[1,4608]{1,0:T(1,128)} reshape(f32[4608]{0:T(1024)} %param.9) | data formatting | bytes 36864 | tf_op jit(solution)/shard_map/reshape | solution.py:426
  1.3 60.8 %shard_map.82 = (bf16[8,48,256]{2,1,0:T(8,128)(2,1)}, bf16[8,512]{1,0:T(8,128)(2,1)}) custom-call(bf16[2,16,4608]{2,1,0:T(8,128)(2,1)} %tok_ref.1, f32[1,4608]{1,0:T(1,128)} %reshape.9.gain_ref, bf16[4608,1536]{1,0:T(8,128)(2,1)} %wq_hbm.1, bf16[4608,512]{1,0:T(8,128)(2,1)} %wkv_hbm.1), custom_call_target="tpu_custom_call" | custom-call | tf_op jit(solution)/shard_map/pallas_call | solution.py:392
  62.1 7.6 %shard_map.83 = bf16[384,256]{1,0:T(8,128)(2,1)} custom-call(s32[4]{0:T(128)} %lens_ref.1, bf16[384,256]{1,0:T(8,128)(2,1)} %bitcast.3, bf16[8,512]{1,0:T(8,128)(2,1)} %get-tuple-element.8.kv_ref, bf16[4,2048,256]{2,1,0:T(8,128)(2,1)} %k_ref.1, bf16[4,2048,256]{2,1,0:T(8,128)(2,1)} %v_ref.1), custom_call_target="tpu_custom_call" | custom-call | tf_op jit(solution)/shard_map/pallas_call | solution.py:72
  69.7 39.1 %shard_map.84 = bf16[2,16,4608]{2,1,0:T(8,128)(2,1)} custom-call(bf16[8,48,256]{2,1,0:T(8,128)(2,1)} %bitcast.2, bf16[1536,4608]{1,0:T(8,128)(2,1)} %w_hbm.1), custom_call_target="tpu_custom_call" | custom-call | tf_op jit(solution)/shard_map/pallas_call | solution.py:593
  108.8 1.7 %copy.10 = bf16[2,16,4608]{2,1,0:T(8,128)(2,1)} copy(bf16[2,16,4608]{2,1,0:T(8,128)(2,1)} %shard_map.84) | data formatting | bytes 589824

commit v4 on v3

--- a/solution.py
+++ b/solution.py
@@ -21,8 +21,16 @@
         q_f[0] = q_ref[:, :128].astype(jnp.float32)
         q_f[1] = q_ref[:, 128:].astype(jnp.float32)
 
-    picked = pl.ds(r, n, stride=4)
-    q = jnp.concatenate([q_f[0, picked, :], q_f[1, picked, :]], axis=1).astype(jnp.bfloat16)
+    heads = n // STEPS
+    q = jnp.concatenate(
+        [
+            jnp.concatenate(
+                [q_f[c, pl.ds(t * 4 + r, heads, stride=8), :] for c in range(2)], axis=1
+            )
+            for t in range(STEPS)
+        ],
+        axis=0,
+    ).astype(jnp.bfloat16)
     factor = HEAD_DIM ** (-0.5)
     s = lax.dot_general(
         q, k_ref[0], (((1,), (1,)), ((), ())), preferred_element_type=jnp.float32
@@ -40,7 +48,7 @@
         jnp.sum(q32 * fresh[t][:, :HEAD_DIM], axis=1, keepdims=True) * factor
         for t in range(STEPS)
     ]
-    step = lax.broadcasted_iota(jnp.int32, (n, 1), 0) % STEPS
+    step = lax.broadcasted_iota(jnp.int32, (n, 1), 0) // heads
     for t in range(1, STEPS):
         new[t] = jnp.where(step >= t, new[t], -1e30)
     top = jnp.max(s, axis=1, keepdims=True)
@@ -57,13 +65,15 @@
     for t in range(STEPS):
         wt = (e_new[t] * inv).astype(jnp.bfloat16).astype(jnp.float32)
         out = out + wt * fresh[t][:, HEAD_DIM:]
-    o_f[0, picked, :] = out[:, :128]
-    o_f[1, picked, :] = out[:, 128:]
+    for t in range(STEPS):
+        for c in range(2):
+            o_f[t, pl.ds(c * 4 + r, heads, stride=8), :] = out[
+                t * heads : (t + 1) * heads, c * 128 : (c + 1) * 128
+            ]
 
     @pl.when(r == rows - 1)
     def _():
-        o_ref[:, :128] = o_f[0].astype(jnp.bfloat16)
-        o_ref[:, 128:] = o_f[1].astype(jnp.bfloat16)
+        o_ref[...] = o_f[...].astype(jnp.bfloat16)
 
 
 def attend(lens, q, kv, keys, values):
@@ -72,7 +82,7 @@
     return pl.pallas_call(
         attend_kernel,
         grid=(rows,),
-        out_shape=jax.ShapeDtypeStruct(q.shape, jnp.bfloat16),
+        out_shape=jax.ShapeDtypeStruct((STEPS, q.shape[0], 128), jnp.bfloat16),
         in_specs=[
             pl.BlockSpec(memory_space=pltpu.SMEM),
             whole(q),
@@ -80,7 +90,7 @@
             pl.BlockSpec((1, cache, dim), lambda r: (r, 0, 0)),
             pl.BlockSpec((1, cache, dim), lambda r: (r, 0, 0)),
         ],
-        out_specs=whole(q),
+        out_specs=pl.BlockSpec((STEPS, q.shape[0], 128), lambda r: (0, 0, 0)),
         scratch_shapes=[
             pltpu.VMEM((2, q.shape[0], 128), jnp.float32),
             pltpu.VMEM((2, q.shape[0], 128), jnp.float32),
@@ -278,7 +288,7 @@
         def _():
             product(it)
 
-        ur = it - gx
+        ur = it - 2 * gx
 
         @pl.when((ur >= 0) & (ur < units))
         def _():
@@ -292,7 +302,7 @@
 
                     go_right(ur, g).start()
 
-        ul = it - (last - gx)
+        ul = it - 2 * (last - gx)
 
         @pl.when((ul >= 0) & (ul < units))
         def _():
@@ -312,7 +322,7 @@
 
         return carry
 
-    lax.fori_loop(0, units + last, one, 0)
+    lax.fori_loop(0, units + 2 * last, one, 0)
 
     def finish(h, carry):
         got = []
@@ -427,16 +437,17 @@
 
 
 def output_kernel(
-    n_gx, n_gy, pack,
+    n_gx, n_gy, local,
     m_ref, w_hbm, o_ref,
-    w, ab, x2f, x2b, pb, sb, keep, psum, rb, of,
-    w_sem, aa_s, aa_r, ri_s, ri_r, le_s, le_r, sib_s, sib_r, rs_s, rs_r,
+    w, ab, x2f, x2b, pb, sb, keep, psum, rb,
+    w_sem, aa_s, aa_r, ag_s, ag_r, sib_s, sib_r, rs_s, rs_r,
 ):
     gx, gy = lax.axis_index("gx"), lax.axis_index("gy")
     tile = w.shape[2]
-    heads = m_ref.shape[1] // pack
+    pieces = m_ref.shape[2] // local
     half = n_gy // 2
-    mine = x2f.shape[0] // n_gy
+    mine = o_ref.shape[1]
+    units = STEPS * NT
     odd = lax.rem(gy, 2)
     sib = gy + 1 - 2 * odd
 
@@ -451,167 +462,135 @@
 
     here = gx * n_gy + gy
     sends = []
-    for o in range(1, n_gy):
-        dst = turn(gy + o, n_gy)
-        c = remote(m_ref.at[dst], ab.at[here], aa_s.at[o], aa_r.at[o], (gx, dst))
-        c.start()
-        sends.append(c)
-    ab[here] = m_ref[gy]
-    last = n_gx - 1
-
-    def right(o, e):
-        slot = (gx - e) * n_gy + turn(gy - o, n_gy)
-        return remote(
-            ab.at[slot], ab.at[slot], ri_s.at[o, e], ri_r.at[o, e], (turn(gx + 1, n_gx), gy)
-        )
-
-    def left(o, e):
-        slot = (gx + e) * n_gy + turn(gy - o, n_gy)
-        return remote(
-            ab.at[slot], ab.at[slot], le_s.at[o, e], le_r.at[o, e], (turn(gx - 1, n_gx), gy)
-        )
-
-    def came_right(o, e):
-        slot = (gx - e) * n_gy + turn(gy - o, n_gy)
-        return remote(
-            ab.at[slot], ab.at[slot], ri_s.at[o, e - 1], ri_r.at[o, e - 1],
-            (turn(gx - 1, n_gx), gy),
-        )
-
-    def came_left(o, e):
-        slot = (gx + e) * n_gy + turn(gy - o, n_gy)
-        return remote(
-            ab.at[slot], ab.at[slot], le_s.at[o, e - 1], le_r.at[o, e - 1],
-            (turn(gx + 1, n_gx), gy),
-        )
-
-    for e in range(n_gx):
+    for s in range(STEPS):
+        for o in range(1, n_gy):
+            dst = turn(gy + o, n_gy)
+            c = remote(
+                m_ref.at[s, dst], ab.at[s, here], aa_s.at[s, o], aa_r.at[s, o], (gx, dst)
+            )
+            c.start()
+            sends.append(c)
+        ab[s, here] = m_ref[s, gy]
+    for s in range(STEPS):
         for o in range(n_gy):
-            if e == 0 and o > 0:
-                src = turn(gy - o, n_gy)
-                slot = gx * n_gy + src
-                remote(ab.at[slot], ab.at[slot], aa_s.at[o], aa_r.at[o], (gx, src)).wait_recv()
-
-            @pl.when(gx >= e)
-            def _():
-                if e > 0:
-                    came_right(o, e).wait_recv()
-
-                @pl.when(gx < last)
-                def _():
-                    right(o, e).start()
-
-            @pl.when(gx + e <= last)
-            def _():
-                if e > 0:
-                    came_left(o, e).wait_recv()
-
-                @pl.when(gx > 0)
-                def _():
-                    left(o, e).start()
-
-    def place(g, carry):
-        got = ab[g].astype(jnp.float32)
-        for h in range(heads):
-            x2f[pl.ds(pl.multiple_of(g * pack, pack), pack), h * HEAD_DIM : (h + 1) * HEAD_DIM] = (
-                got[h * pack : (h + 1) * pack]
-            )
-        return carry
-
-    lax.fori_loop(0, n_gx * n_gy, place, 0)
-    x2b[...] = x2f[...].astype(jnp.bfloat16)
-
-    def to_sib(t):
-        return remote(pb.at[t, :, 1 - odd], sb.at[t], sib_s.at[t], sib_r.at[t], (gx, sib))
-
-    def multiply(t):
-        load(t).wait()
-        part = jnp.dot(x2b[...], w[t], preferred_element_type=jnp.float32).astype(jnp.bfloat16)
-        pb[t] = part.reshape(half, 2, mine, tile)
-        to_sib(t).start()
-
-    def to_peer(t, o):
+            src = turn(gy - o, n_gy)
+            slot = ab.at[s, gx * n_gy + src]
+            if o > 0:
+                remote(slot, slot, aa_s.at[s, o], aa_r.at[s, o], (gx, src)).wait_recv()
+            for p in range(1, n_gx):
+                c = remote(
+                    slot, slot, ag_s.at[s, o, p], ag_r.at[s, o, p], (turn(gx + p, n_gx), gy)
+                )
+                c.start()
+                sends.append(c)
+
+    def gathered(s):
+        for o in range(n_gy):
+            for p in range(1, n_gx):
+                src = turn(gx - p, n_gx)
+                slot = ab.at[s, src * n_gy + turn(gy - o, n_gy)]
+                remote(slot, slot, ag_s.at[s, o, p], ag_r.at[s, o, p], (src, gy)).wait_recv()
+
+        def place(g, carry):
+            got = [ab[s, 2 * g + k].astype(jnp.float32) for k in range(2)]
+            at = pl.ds(pl.multiple_of(g * 2 * local, 2 * local), 2 * local)
+            for k in range(pieces):
+                x2f[at, k * 128 : (k + 1) * 128] = jnp.concatenate(
+                    [y[k * local : (k + 1) * local] for y in got], axis=0
+                )
+            return carry
+
+        lax.fori_loop(0, n_gx * n_gy // 2, place, 0)
+        x2b[s] = x2f[...].astype(jnp.bfloat16)
+
+    def to_sib(u):
+        return remote(pb.at[u, :, 1 - odd], sb.at[u], sib_s.at[u], sib_r.at[u], (gx, sib))
+
+    def multiply(u):
+        s = u // NT
+        t = u - s * NT
+        part = jnp.dot(x2b[s], w[t], preferred_element_type=jnp.float32).astype(jnp.bfloat16)
+        pb[u] = part.reshape(half, 2, mine, tile)
+        to_sib(u).start()
+
+    def to_peer(u, o):
         dst = turn(gy + 2 * o, n_gy)
         return remote(
-            psum.at[t, dst // 2], rb.at[t, o], rs_s.at[t, o], rs_r.at[t, o], (gx, dst)
-        )
-
-    def pair(t):
-        to_sib(t).wait()
-        both = pb[t, :, odd].astype(jnp.float32) + sb[t].astype(jnp.float32)
-        psum[t] = both.astype(jnp.bfloat16)
+            psum.at[u, dst // 2], rb.at[u, o], rs_s.at[u, o], rs_r.at[u, o], (gx, dst)
+        )
+
+    def pair(u):
+        to_sib(u).wait()
+        both = pb[u, :, odd].astype(jnp.float32) + sb[u].astype(jnp.float32)
+        psum[u] = both.astype(jnp.bfloat16)
         for o in range(1, half):
-            to_peer(t, o).start()
-        keep[t] = pb[t, gy // 2, odd].astype(jnp.float32) + sb[t, gy // 2].astype(jnp.float32)
-
-    multiply(0)
-
-    def stage(t, carry):
-        multiply(t)
-        pair(t - 1)
+            to_peer(u, o).start()
+        keep[u] = pb[u, gy // 2, odd].astype(jnp.float32) + sb[u, gy // 2].astype(jnp.float32)
+
+    gathered(0)
+    for u in range(2):
+        load(u).wait()
+        multiply(u)
+
+    def stage(u, carry):
+        pair(u - 2)
+
+        @pl.when(u == NT)
+        def _():
+            gathered(1)
+
+        @pl.when(u < NT)
+        def _():
+            load(u).wait()
+
+        multiply(u)
         return carry
 
-    lax.fori_loop(1, NT, stage, 0)
-    pair(NT - 1)
-
-    local = pack // STEPS
-    for t in range(NT):
-        out = keep[t]
+    lax.fori_loop(2, units, stage, 0)
+    pair(units - 2)
+    pair(units - 1)
+
+    for u in range(units):
+        out = keep[u]
         for o in range(1, half):
-            to_peer(t, o).wait()
-            out = out + rb[t, o].astype(jnp.float32)
-        for f in range(mine // pack):
-            for s in range(STEPS):
-                of[s, f * local : (f + 1) * local, t * tile : (t + 1) * tile] = (
-                    out[f * pack + s * local : f * pack + (s + 1) * local]
-                )
-    o_ref[...] = of[...].astype(jnp.bfloat16)
-    for e in range(n_gx):
-        for o in range(n_gy):
-            @pl.when((gx >= e) & (gx < last))
-            def _():
-                right(o, e).wait_send()
-
-            @pl.when((gx + e <= last) & (gx > 0))
-            def _():
-                left(o, e).wait_send()
-
+            to_peer(u, o).wait()
+            out = out + rb[u, o].astype(jnp.float32)
+        t = u % NT
+        o_ref[u // NT, :, t * tile : (t + 1) * tile] = out.astype(jnp.bfloat16)
     for c in sends:
         c.wait_send()
 
 
 def project_out(n_gx, n_gy, local, mixed, w_out):
-    pack = STEPS * local
     depth, width = w_out.shape
     tile = width // NT
-    rows = n_gx * n_gy * pack
+    rows = n_gx * n_gy * local
     mine = rows // n_gy
     half = n_gy // 2
+    units = STEPS * NT
     dma = pltpu.SemaphoreType.DMA
     bf, f32 = jnp.bfloat16, jnp.float32
     vmem = pl.BlockSpec(memory_space=pltpu.VMEM)
     return pl.pallas_call(
-        functools.partial(output_kernel, n_gx, n_gy, pack),
-        out_shape=jax.ShapeDtypeStruct((STEPS, mine // STEPS, width), bf),
+        functools.partial(output_kernel, n_gx, n_gy, local),
+        out_shape=jax.ShapeDtypeStruct((STEPS, mine, width), bf),
         in_specs=[vmem, pl.BlockSpec(memory_space=pl.ANY)],
         out_specs=vmem,
         scratch_shapes=[
             pltpu.VMEM((NT, depth, tile), bf),
-            pltpu.VMEM((n_gx * n_gy,) + mixed.shape[1:], bf),
+            pltpu.VMEM((STEPS, n_gx * n_gy) + mixed.shape[2:], bf),
             pltpu.VMEM((rows, depth), f32),
-            pltpu.VMEM((rows, depth), bf),
-            pltpu.VMEM((NT, half, 2, mine, tile), bf),
-            pltpu.VMEM((NT, half, mine, tile), bf),
-            pltpu.VMEM((NT, mine, tile), f32),
-            pltpu.VMEM((NT, half, mine, tile), bf),
-            pltpu.VMEM((NT, half, mine, tile), bf),
-            pltpu.VMEM((STEPS, mine // STEPS, width), f32),
+            pltpu.VMEM((STEPS, rows, depth), bf),
+            pltpu.VMEM((units, half, 2, mine, tile), bf),
+            pltpu.VMEM((units, half, mine, tile), bf),
+            pltpu.VMEM((units, mine, tile), f32),
+            pltpu.VMEM((units, half, mine, tile), bf),
+            pltpu.VMEM((units, half, mine, tile), bf),
             dma((NT,)),
-            dma((n_gy,)), dma((n_gy,)),
-            dma((n_gy, n_gx)), dma((n_gy, n_gx)),
-            dma((n_gy, n_gx)), dma((n_gy, n_gx)),
-            dma((NT,)), dma((NT,)),
-            dma((NT, half)), dma((NT, half)),
+            dma((STEPS, n_gy)), dma((STEPS, n_gy)),
+            dma((STEPS, n_gy, n_gx)), dma((STEPS, n_gy, n_gx)),
+            dma((units,)), dma((units,)),
+            dma((units, half)), dma((units, half)),
         ],
         compiler_params=pltpu.CompilerParams(
             collective_id=1, has_side_effects=True, vmem_limit_bytes=56 * 2**20
@@ -623,7 +602,7 @@
     local = keys.shape[0]
     q, kv = project(d, n_gx, n_gy, local, tokens, norm_gain, w_query, w_kv)
     mixed = attend(lengths, q.reshape(-1, HEAD_DIM), kv, keys, values)
-    return project_out(n_gx, n_gy, local, mixed.reshape(q.shape), w_out)
+    return project_out(n_gx, n_gy, local, mixed.reshape(STEPS, n_gy, -1, 128), w_out)
 
 
 def solution(mesh):

time: 111 us -> 109 us (0.982)
    pallas_call x1, Pallas kernels: 39.1 us -> 37.9 us  [project_out(): pl.pallas_call(functools.partial(output_kernel, n_gx, n_gy, local), out_s...]
where the time goes in v4:
time: 109 us
  Pallas kernels  106 us (97%)
  local copies, waits for them, and re-layouts  3.04 us (3%)
    pallas_call x1, Pallas kernels, project(): pl.pallas_call(functools.partial(project_kernel, d, n_gx, n_gy), out_shap...  60.6 us
    pallas_call x1, Pallas kernels, project_out(): pl.pallas_call(functools.partial(output_kernel, n_gx, n_gy, local), out_s...  37.9 us
    pallas_call x1, Pallas kernels, attend(): pl.pallas_call(attend_kernel, grid=(rows,), out_shape=jax.ShapeDtypeStruc...  7.57 us

profile of v4, /device:TPU:0, one launch (start us, length us, event | category | flops | bytes accessed | tf_op | source)
XLA Modules:
  0.0 109.0 jit_solution(10331454002365716784)
XLA Ops:
  0.0 1.3 %reshape.9.gain_ref = f32[1,4608]{1,0:T(1,128)} reshape(f32[4608]{0:T(1024)} %param.9) | data formatting | bytes 36864 | tf_op jit(solution)/shard_map/reshape | solution.py:436
  1.3 60.6 %shard_map.82 = (bf16[8,48,256]{2,1,0:T(8,128)(2,1)}, bf16[8,512]{1,0:T(8,128)(2,1)}) custom-call(bf16[2,16,4608]{2,1,0:T(8,128)(2,1)} %tok_ref.1, f32[1,4608]{1,0:T(1,128)} %reshape.9.gain_ref, bf16[4608,1536]{1,0:T(8,128)(2,1)} %wq_hbm.1, bf16[4608,512]{1,0:T(8,128)(2,1)} %wkv_hbm.1), custom_call_target="tpu_custom_call" | custom-call | tf_op jit(solution)/shard_map/pallas_call | solution.py:402
  61.9 7.6 %shard_map.83 = bf16[2,384,128]{2,1,0:T(8,128)(2,1)} custom-call(s32[4]{0:T(128)} %lens_ref.1, bf16[384,256]{1,0:T(8,128)(2,1)} %bitcast.3, bf16[8,512]{1,0:T(8,128)(2,1)} %get-tuple-element.8.kv_ref, bf16[4,2048,256]{2,1,0:T(8,128)(2,1)} %k_ref.1, bf16[4,2048,256]{2,1,0:T(8,128)(2,1)} %v_ref.1), custom_call_target="tpu_custom_call" | custom-call | tf_op jit(solution)/shard_map/pallas_call | solution.py:82
  69.5 37.9 %shard_map.84 = bf16[2,16,4608]{2,1,0:T(8,128)(2,1)} custom-call(bf16[2,8,48,128]{3,2,1,0:T(8,128)(2,1)} %bitcast.2, bf16[1536,4608]{1,0:T(8,128)(2,1)} %w_hbm.1), custom_call_target="tpu_custom_call" | custom-call | tf_op jit(solution)/shard_map/pallas_call | solution.py:574
  107.3 1.7 %copy.10 = bf16[2,16,4608]{2,1,0:T(8,128)(2,1)} copy(bf16[2,16,4608]{2,1,0:T(8,128)(2,1)} %shard_map.84) | data formatting | bytes 589824

commit v5 on v4

--- a/solution.py
+++ b/solution.py
@@ -189,6 +189,11 @@
     def to_sib(s):
         return remote(xg.at[s, gy], xg.at[s, gy], sb_s.at[s], sb_r.at[s], (gx, sib))
 
+    def share(s):
+        for o in range(1, half):
+            to_chip(s, o).start()
+        to_sib(s).start()
+
     def pass_on(s, o):
         src = turn(gy - 2 * o, n_gy)
         return remote(xg.at[s, src], xg.at[s, src], fw_s.at[s, o], fw_r.at[s, o], (gx, sib))
@@ -215,11 +220,11 @@
         spread = t[:, 64:65] / d - average * average
         normed = (tok_ref[s].astype(jnp.float32) - average) * lax.rsqrt(spread + 1e-05)
         xg[s, gy] = (normed * gain_ref[...]).astype(jnp.bfloat16)
-        for o in range(1, half):
-            to_chip(s, o).start()
-        to_sib(s).start()
+        if s == 0:
+            share(0)
     relay(0)
     arrived(0)
+    share(1)
 
     def send_kv(o):
         dst = turn(gx + o, n_gx)
@@ -316,7 +321,7 @@
 
                     go_left(ul, g).start()
 
-        @pl.when(it == units)
+        @pl.when(it == heads + 1)
         def _():
             fresh()
 
@@ -471,7 +476,7 @@
             c.start()
             sends.append(c)
         ab[s, here] = m_ref[s, gy]
-    for s in range(STEPS):
+    def pass_along(s):
         for o in range(n_gy):
             src = turn(gy - o, n_gy)
             slot = ab.at[s, gx * n_gy + src]
@@ -484,13 +489,14 @@
                 c.start()
                 sends.append(c)
 
-    def gathered(s):
+    def landed(s):
         for o in range(n_gy):
             for p in range(1, n_gx):
                 src = turn(gx - p, n_gx)
                 slot = ab.at[s, src * n_gy + turn(gy - o, n_gy)]
                 remote(slot, slot, ag_s.at[s, o, p], ag_r.at[s, o, p], (src, gy)).wait_recv()
 
+    def gathered(s):
         def place(g, carry):
             got = [ab[s, 2 * g + k].astype(jnp.float32) for k in range(2)]
             at = pl.ds(pl.multiple_of(g * 2 * local, 2 * local), 2 * local)
@@ -527,6 +533,9 @@
             to_peer(u, o).start()
         keep[u] = pb[u, gy // 2, odd].astype(jnp.float32) + sb[u, gy // 2].astype(jnp.float32)
 
+    pass_along(0)
+    landed(0)
+    pass_along(1)
     gathered(0)
     for u in range(2):
         load(u).wait()
@@ -537,6 +546,7 @@
 
         @pl.when(u == NT)
         def _():
+            landed(1)
             gathered(1)
 
         @pl.when(u < NT)

time: 109 us -> 111 us (1.018)
  Pallas kernels: 106 us -> 108 us
    pallas_call x1, Pallas kernels: 37.9 us -> 39 us  [project_out(): pl.pallas_call(functools.partial(output_kernel, n_gx, n_gy, local), out_s...]
where the time goes in v5:
time: 111 us
  Pallas kernels  108 us (97%)
  local copies, waits for them, and re-layouts  3.04 us (3%)
    pallas_call x1, Pallas kernels, project(): pl.pallas_call(functools.partial(project_kernel, d, n_gx, n_gy), out_shap...  61.1 us
    pallas_call x1, Pallas kernels, project_out(): pl.pallas_call(functools.partial(output_kernel, n_gx, n_gy, local), out_s...  39 us
    pallas_call x1, Pallas kernels, attend(): pl.pallas_call(attend_kernel, grid=(rows,), out_shape=jax.ShapeDtypeStruc...  7.58 us

profile of v5, /device:TPU:0, one launch (start us, length us, event | category | flops | bytes accessed | tf_op | source)
XLA Modules:
  0.0 110.8 jit_solution(13432447727496394519)
XLA Ops:
  0.0 1.3 %reshape.9.gain_ref = f32[1,4608]{1,0:T(1,128)} reshape(f32[4608]{0:T(1024)} %param.9) | data formatting | bytes 36864 | tf_op jit(solution)/shard_map/reshape | solution.py:441
  1.3 61.1 %shard_map.82 = (bf16[8,48,256]{2,1,0:T(8,128)(2,1)}, bf16[8,512]{1,0:T(8,128)(2,1)}) custom-call(bf16[2,16,4608]{2,1,0:T(8,128)(2,1)} %tok_ref.1, f32[1,4608]{1,0:T(1,128)} %reshape.9.gain_ref, bf16[4608,1536]{1,0:T(8,128)(2,1)} %wq_hbm.1, bf16[4608,512]{1,0:T(8,128)(2,1)} %wkv_hbm.1), custom_call_target="tpu_custom_call" | custom-call | tf_op jit(solution)/shard_map/pallas_call | solution.py:407
  62.5 7.6 %shard_map.83 = bf16[2,384,128]{2,1,0:T(8,128)(2,1)} custom-call(s32[4]{0:T(128)} %lens_ref.1, bf16[384,256]{1,0:T(8,128)(2,1)} %bitcast.3, bf16[8,512]{1,0:T(8,128)(2,1)} %get-tuple-element.8.kv_ref, bf16[4,2048,256]{2,1,0:T(8,128)(2,1)} %k_ref.1, bf16[4,2048,256]{2,1,0:T(8,128)(2,1)} %v_ref.1), custom_call_target="tpu_custom_call" | custom-call | tf_op jit(solution)/shard_map/pallas_call | solution.py:82
  70.1 39.0 %shard_map.84 = bf16[2,16,4608]{2,1,0:T(8,128)(2,1)} custom-call(bf16[2,8,48,128]{3,2,1,0:T(8,128)(2,1)} %bitcast.2, bf16[1536,4608]{1,0:T(8,128)(2,1)} %w_hbm.1), custom_call_target="tpu_custom_call" | custom-call | tf_op jit(solution)/shard_map/pallas_call | solution.py:584
  109.1 1.7 %copy.10 = bf16[2,16,4608]{2,1,0:T(8,128)(2,1)} copy(bf16[2,16,4608]{2,1,0:T(8,128)(2,1)} %shard_map.84) | data formatting | bytes 589824
